TPU v7x, 128 devices: a whole 4x4x4 slice. The times are simulated.
128 devices in a mesh: batch: 4 (over z), seq: 32 (over x, y, core).
Axes of the slice: x: 4, y: 4, z: 4, core: 2. Of those that a mesh axis runs over, the one named last changes fastest.
Arguments:
- tokens: bfloat16 [8, 2048, 2048], P('batch', 'seq'), may hold values from -6 to 6
- time_weights: bfloat16 [5, 2048, 2048], P(None, ('batch', 'seq')), may hold values from -0.125 to 0.125
- channel_key: bfloat16 [2048, 7168], P(('batch', 'seq')), may hold values from -0.125 to 0.125
- channel_value: bfloat16 [2048, 7168], P(('batch', 'seq')), may hold values from -0.0625 to 0.0625
- channel_gate: bfloat16 [2048, 2048], P(('batch', 'seq')), may hold values from -0.125 to 0.125
- vectors: bfloat16 [13, 2048], P(None, ('batch', 'seq')), may hold values from -1 to 1.5
- head_decay: float32 [32], replicated, may hold values from 0.9 to 1
- lengths: int32 [8], P('batch'), may hold values from 512 to 2048, as said below
- cotangent: bfloat16 [8, 2048, 2048], P('batch', 'seq'), may hold values from -6 to 6
Outputs:
- layer_out: bfloat16 [8, 2048, 2048], P('batch', 'seq')
- token_grad: bfloat16 [8, 2048, 2048], P('batch', 'seq')
- time_grads: float32 [5, 2048, 2048], P(None, ('batch', 'seq'))
- key_grad: float32 [2048, 7168], P(('batch', 'seq'))
- value_grad: float32 [2048, 7168], P(('batch', 'seq'))
- gate_grad: float32 [2048, 2048], P(('batch', 'seq'))
- vector_grads: float32 [13, 2048], P(None, ('batch', 'seq'))
Inputs may be any that keep to these rules, and one draw needn't show every extreme that they name: `lengths`: in each batch group of 2 sequences one, chosen by the seed, has length 2048.
All inputs are finite; a program needn't handle non-finite values.
Results may differ from a plain program's by a relative error of at most 0.02.
Values may be sent and summed in bfloat16 or wider, within the bound.
A program may use at most 640 MiB of HBM per device.

v0:
```python
import jax
import jax.numpy as jnp
from jax import lax
from jax.sharding import PartitionSpec as P

BLOCK_LEN = 64


epsilon = 1e-05
group_epsilon = 0.00064
highest = lax.Precision.HIGHEST


def shifted(block, axis, distance):
    devices = range(lax.axis_size(axis))
    route = [(i - distance, i) for i in devices if i - distance in devices]
    return lax.ppermute(block, axis, route)


def carried_in(array, axis, combine, identity):
    devices, place = (lax.axis_size(axis), lax.axis_index(axis))
    everything = jax.tree.map(lambda part: lax.all_gather(part, axis), array)
    start = jax.tree.map(
        lambda part, zero: jnp.broadcast_to(jnp.asarray(zero, part.dtype), part.shape),
        array,
        identity,
    )

    def carried_lap(k, before):
        reached = k < place
        new = combine(before, jax.tree.map(lambda part: part[k], everything))
        return jax.tree.map(lambda a, b: jnp.where(reached, a, b), new, before)

    return lax.fori_loop(0, devices, carried_lap, start)


def entering_2(array, axis, combine, identity):
    devices, place = (lax.axis_size(axis), lax.axis_index(axis))
    everything = jax.tree.map(
        lambda part, kind: lax.all_gather(part.astype(kind), axis),
        array,
        (jnp.bfloat16, jnp.bfloat16),
    )
    start = jax.tree.map(
        lambda part, zero: jnp.broadcast_to(jnp.asarray(zero, part.dtype), part.shape),
        array,
        identity,
    )

    def entering_lap(k, before):
        at = devices - 1 - k
        reached = at > place
        new = combine(
            before, jax.tree.map(lambda part, own: part[at].astype(own.dtype), everything, array)
        )
        return jax.tree.map(lambda a, b: jnp.where(reached, a, b), new, before)

    return lax.fori_loop(0, devices, entering_lap, start)


def layer_norm(values, gain_row, offset):
    center = values - jnp.mean(values, axis=-1, keepdims=True)
    inverse = lax.rsqrt(jnp.mean(center * center, axis=-1, keepdims=True) + epsilon)
    scaled = center * inverse
    return (scaled * gain_row + offset, scaled, inverse)


def norm_back(upstream, scaled, inverse, gain_row):
    inner_grad = upstream * gain_row
    return inverse * (
        inner_grad
        - jnp.mean(inner_grad, axis=-1, keepdims=True)
        - scaled * jnp.mean(inner_grad * scaled, axis=-1, keepdims=True)
    )


def matmul_right(left_mat, right_mat):
    return lax.dot_general(
        left_mat, right_mat, (((1,), (1,)), ((), ())), preferred_element_type=jnp.float32
    )


def chain_state(earlier, later):
    return (earlier[0] * later[0], earlier[1] * later[0][None, :, None, None] + later[1])


def body(
    tokens,
    time_weights,
    channel_key,
    channel_value,
    channel_gate,
    vectors,
    head_decay,
    lengths,
    cotangent,
):
    groups, span_len, model_width = tokens.shape
    attention_tally = head_decay.shape[0]
    attention_dimension = model_width // attention_tally
    blocks = span_len // BLOCK_LEN
    row_count = groups * span_len
    features = channel_key.shape[1]
    local_rows = channel_key.shape[0]
    own_place = lax.axis_index("seq")
    fading_exponent = jnp.log(head_decay)
    places = jnp.arange(BLOCK_LEN, dtype=jnp.float32)
    below = places[:, None] > places[None, :]
    spread = jnp.where(below, places[:, None] - 1.0 - places[None, :], 0.0)
    mask_table = jnp.where(below[None], jnp.exp(spread[None] * fading_exponent[:, None, None]), 0.0)
    enter_decay = jnp.exp(places[:, None] * fading_exponent[None, :])
    leave_decay = jnp.exp((BLOCK_LEN - 1.0 - places)[:, None] * fading_exponent[None, :])
    block_decay = jnp.exp(BLOCK_LEN * fading_exponent)
    block_powers = jnp.exp(
        BLOCK_LEN * jnp.arange(blocks, dtype=jnp.float32)[:, None] * fading_exponent[None, :]
    )
    device_log = span_len * fading_exponent
    device_decay = jnp.exp(device_log)
    identity_mat = jnp.eye(BLOCK_LEN, dtype=jnp.float32)
    time_full, vector_full = (
        lax.all_gather(time_weights, ("batch", "seq"), axis=1, tiled=True),
        lax.all_gather(vectors, ("batch", "seq"), axis=1, tiled=True),
    )
    learned_settings = vector_full.astype(jnp.float32)
    attention_reward = learned_settings[6].reshape(attention_tally, attention_dimension)
    inputs = tokens.astype(jnp.float32)
    first_norm, first_scaled, first_inverse = layer_norm(
        inputs, learned_settings[0], learned_settings[1]
    )
    first_edge = shifted(first_norm[:, -1, :], "seq", 1)
    first_prev = jnp.concatenate([first_edge[:, None, :], first_norm[:, :-1, :]], axis=1)
    first_delta = (first_norm - first_prev).reshape(row_count, model_width)
    first_prev = first_prev.reshape(row_count, model_width)
    mix_low = (first_prev[None] + learned_settings[2:6, None, :] * first_delta[None]).astype(
        jnp.bfloat16
    )
    projected = jnp.einsum(
        "prd,pde->pre", mix_low, time_full[:4], preferred_element_type=jnp.float32
    )
    gate_pre = projected[3]
    gate_act = jax.nn.silu(gate_pre)
    block_shape = (groups, blocks, BLOCK_LEN, attention_tally, attention_dimension)
    recv_low = projected[0].astype(jnp.bfloat16).reshape(block_shape)
    key_low = projected[1].astype(jnp.bfloat16).reshape(block_shape)
    value_low = projected[2].astype(jnp.bfloat16).reshape(block_shape)
    acceptor_expanded = recv_low.astype(jnp.float32)
    lookup_expanded = key_low.astype(jnp.float32)
    value_wide = value_low.astype(jnp.float32)
    scores = jnp.einsum("snihe,snjhe->snhij", recv_low, key_low, preferred_element_type=jnp.float32)
    self_pair_contribution = jnp.sum(
        acceptor_expanded * attention_reward * lookup_expanded, axis=-1
    )
    weights_low = (
        scores * mask_table + identity_mat * jnp.swapaxes(self_pair_contribution, 2, 3)[..., None]
    ).astype(jnp.bfloat16)
    intra_out = jnp.einsum(
        "snhij,snjhe->snihe", weights_low, value_low, preferred_element_type=jnp.float32
    )
    key_leave = lookup_expanded * leave_decay[:, :, None]
    block_states = jnp.einsum("snjhe,snjhf->snhef", key_leave, value_wide, precision=highest)
    running = jnp.zeros(
        (groups, attention_tally, attention_dimension, attention_dimension), jnp.float32
    )
    block_index = 0
    prefixes = [running]
    running = running * block_decay[None, :, None, None] + block_states[:, block_index]
    local_total = running
    carried_decay, entering = carried_in(
        (device_decay, local_total),
        "seq",
        chain_state,
        (jnp.ones_like(device_decay), jnp.zeros_like(local_total)),
    )
    incoming = entering[:, None] * block_powers[None, :, :, None, None] + jnp.stack(
        prefixes, axis=1
    )
    recv_enter = acceptor_expanded * enter_decay[:, :, None]
    carried_out = jnp.einsum("snihe,snhef->snihf", recv_enter, incoming, precision=highest)
    wkv_out = (intra_out + carried_out).reshape(row_count, attention_tally, attention_dimension)
    wkv_center = wkv_out - jnp.mean(wkv_out, axis=-1, keepdims=True)
    wkv_inverse = lax.rsqrt(
        jnp.mean(wkv_center * wkv_center, axis=-1, keepdims=True) + group_epsilon
    )
    wkv_scaled = wkv_center * wkv_inverse
    normed = wkv_scaled.reshape(row_count, model_width) * learned_settings[7] + learned_settings[8]
    gated_low = (normed * gate_act).astype(jnp.bfloat16)
    hidden_one = inputs.reshape(row_count, model_width) + jnp.dot(
        gated_low, time_full[4], preferred_element_type=jnp.float32
    )
    key_full, value_full, gate_full = (
        lax.all_gather(channel_key, ("batch", "seq"), axis=0, tiled=True),
        lax.all_gather(channel_value, ("batch", "seq"), axis=0, tiled=True),
        lax.all_gather(channel_gate, ("batch", "seq"), axis=0, tiled=True),
    )
    second, second_scaled, second_inverse = layer_norm(
        hidden_one.reshape(groups, span_len, model_width), learned_settings[9], learned_settings[10]
    )
    second_edge = shifted(second[:, -1, :], "seq", 1)
    second_prev = jnp.concatenate([second_edge[:, None, :], second[:, :-1, :]], axis=1)
    second_delta = (second - second_prev).reshape(row_count, model_width)
    second_prev = second_prev.reshape(row_count, model_width)
    ckey = (second_prev + learned_settings[11] * second_delta).astype(jnp.bfloat16)
    cgate = (second_prev + learned_settings[12] * second_delta).astype(jnp.bfloat16)
    key_pre = jnp.dot(ckey, key_full, preferred_element_type=jnp.float32)
    rectified = jax.nn.relu(key_pre)
    hidden = (rectified * rectified).astype(jnp.bfloat16)
    value_out = matmul_right(hidden, value_full)
    gate_sig = jax.nn.sigmoid(jnp.dot(cgate, gate_full, preferred_element_type=jnp.float32))
    layer_out = (
        (hidden_one + gate_sig * value_out)
        .reshape(groups, span_len, model_width)
        .astype(jnp.bfloat16)
    )
    offsets = own_place * span_len + jnp.arange(span_len, dtype=jnp.int32)
    valid_mask = (offsets[None, :] < lengths[:, None]).astype(jnp.float32)
    upstream = (cotangent.astype(jnp.float32) * valid_mask[:, :, None]).reshape(
        row_count, model_width
    )
    key_back, value_back, gate_back = (key_full, value_full, gate_full)
    grad_value = (upstream * gate_sig).astype(jnp.bfloat16)
    grad_gate = (upstream * value_out * gate_sig * (1.0 - gate_sig)).astype(jnp.bfloat16)
    grad_hidden = jnp.dot(grad_value, value_back, preferred_element_type=jnp.float32)
    grad_key = (2.0 * grad_hidden * rectified).astype(jnp.bfloat16)
    channel_left = jnp.stack([ckey, grad_value])
    channel_right = jnp.stack([grad_key, hidden])
    channel_sum = lax.psum_scatter(
        jnp.einsum(
            "prd,prf->dpf", channel_left, channel_right, preferred_element_type=jnp.float32
        ).reshape(local_rows * lax.axis_size(("batch", "seq")), 2 * features),
        ("batch", "seq"),
        scatter_dimension=0,
        tiled=True,
    )
    grad_ckey = matmul_right(grad_key, key_back)
    grad_cgate = matmul_right(grad_gate, gate_back)
    mix_key_grad = jnp.sum(second_delta * grad_ckey, axis=0)
    mix_gate_grad = jnp.sum(second_delta * grad_cgate, axis=0)
    grad_second = (learned_settings[11] * grad_ckey + learned_settings[12] * grad_cgate).reshape(
        groups, span_len, model_width
    )
    grad_second_prev = (
        (1.0 - learned_settings[11]) * grad_ckey + (1.0 - learned_settings[12]) * grad_cgate
    ).reshape(groups, span_len, model_width)
    second_back = shifted(grad_second_prev[:, 0, :], "seq", -1)
    grad_second = grad_second + jnp.concatenate(
        [grad_second_prev[:, 1:, :], second_back[:, None, :]], axis=1
    )
    second_gain_grad = jnp.sum(grad_second * second_scaled, axis=(0, 1))
    second_bias_grad = jnp.sum(grad_second, axis=(0, 1))
    grad_hidden_one = upstream + norm_back(
        grad_second, second_scaled, second_inverse, learned_settings[9]
    ).reshape(row_count, model_width)
    grad_out = grad_hidden_one.astype(jnp.bfloat16)
    grad_gated = matmul_right(grad_out, time_full[4])
    grad_normed = grad_gated * gate_act
    gate_sigma = jax.nn.sigmoid(gate_pre)
    grad_gate_pre = (
        grad_gated * normed * gate_sigma * (1.0 + gate_pre * (1.0 - gate_sigma))
    ).astype(jnp.bfloat16)
    norm_gain_grad = jnp.sum(grad_normed * wkv_scaled.reshape(row_count, model_width), axis=0)
    norm_bias_grad = jnp.sum(grad_normed, axis=0)
    grad_wkv = norm_back(
        grad_normed.reshape(row_count, attention_tally, attention_dimension),
        wkv_scaled,
        wkv_inverse,
        learned_settings[7].reshape(attention_tally, attention_dimension),
    )
    grad_wkv = grad_wkv.astype(jnp.bfloat16).reshape(block_shape)
    grad_wide = grad_wkv.astype(jnp.float32)
    grad_weights = jnp.einsum(
        "snihf,snjhf->snhij", grad_wkv, value_low, preferred_element_type=jnp.float32
    ).astype(jnp.bfloat16)
    grad_weights_wide = grad_weights.astype(jnp.float32)
    masked = grad_weights_wide * mask_table
    acceptor_adjoint = jnp.einsum("snhij,snjhe->snihe", masked, lookup_expanded, precision=highest)
    lookup_adjoints = jnp.einsum("snhij,snihe->snjhe", masked, acceptor_expanded, precision=highest)
    self_pair_adjoint = jnp.swapaxes(jnp.diagonal(grad_weights_wide, axis1=3, axis2=4), 2, 3)
    acceptor_adjoint = (
        acceptor_adjoint + self_pair_adjoint[..., None] * attention_reward * lookup_expanded
    )
    lookup_adjoints = (
        lookup_adjoints + self_pair_adjoint[..., None] * attention_reward * acceptor_expanded
    )
    reward_adjoint = jnp.sum(
        self_pair_adjoint[..., None] * acceptor_expanded * lookup_expanded, axis=(0, 1, 2)
    ).reshape(model_width)
    grad_values = jnp.einsum(
        "snhij,snihf->snjhf", weights_low, grad_wkv, preferred_element_type=jnp.float32
    )
    acceptor_adjoint = (
        acceptor_adjoint
        + jnp.einsum("snihf,snhef->snihe", grad_wide, incoming, precision=highest)
        * enter_decay[:, :, None]
    )
    grad_incoming = jnp.einsum("snihe,snihf->snhef", recv_enter, grad_wide, precision=highest)
    grad_entering = jnp.sum(grad_incoming * block_powers[None, :, :, None, None], axis=1)
    leaving_decay, grad_leaving = entering_2(
        (device_decay, grad_entering),
        "seq",
        chain_state,
        (jnp.ones_like(device_decay), jnp.zeros_like(grad_entering)),
    )
    grad_blocks = [grad_leaving] * blocks
    running = grad_leaving
    for block_index in reversed(range(blocks)):
        grad_blocks[block_index] = running
        running = running * block_decay[None, :, None, None] + grad_incoming[:, block_index]
    grad_states = jnp.stack(grad_blocks, axis=1)
    lookup_adjoints = (
        lookup_adjoints
        + jnp.einsum("snjhf,snhef->snjhe", value_wide, grad_states, precision=highest)
        * leave_decay[:, :, None]
    )
    grad_values = grad_values + jnp.einsum(
        "snjhe,snhef->snjhf", key_leave, grad_states, precision=highest
    )
    grad_proj = jnp.stack(
        [
            acceptor_adjoint.reshape(row_count, model_width).astype(jnp.bfloat16),
            lookup_adjoints.reshape(row_count, model_width).astype(jnp.bfloat16),
            grad_values.reshape(row_count, model_width).astype(jnp.bfloat16),
            grad_gate_pre,
        ]
    )
    grad_mix = jnp.einsum(
        "pre,pde->prd", grad_proj, time_full[:4], preferred_element_type=jnp.float32
    )
    mix_grads = jnp.sum(first_delta[None] * grad_mix, axis=1)
    grad_first = jnp.sum(learned_settings[2:6, None, :] * grad_mix, axis=0).reshape(
        groups, span_len, model_width
    )
    grad_first_prev = jnp.sum((1.0 - learned_settings[2:6, None, :]) * grad_mix, axis=0).reshape(
        groups, span_len, model_width
    )
    first_back = shifted(grad_first_prev[:, 0, :], "seq", -1)
    grad_first = grad_first + jnp.concatenate(
        [grad_first_prev[:, 1:, :], first_back[:, None, :]], axis=1
    )
    first_gain_grad = jnp.sum(grad_first * first_scaled, axis=(0, 1))
    first_bias_grad = jnp.sum(grad_first, axis=(0, 1))
    grad_inputs = grad_hidden_one.reshape(groups, span_len, model_width) + norm_back(
        grad_first, first_scaled, first_inverse, learned_settings[0]
    )
    token_grad = grad_inputs.astype(jnp.bfloat16)
    square_left = jnp.concatenate([mix_low, gated_low[None], cgate[None]], axis=0)
    square_right = jnp.concatenate([grad_proj, grad_out[None], grad_gate[None]], axis=0)
    vector_term = jnp.stack(
        [
            first_gain_grad,
            first_bias_grad,
            mix_grads[0],
            mix_grads[1],
            mix_grads[2],
            mix_grads[3],
            reward_adjoint,
            norm_gain_grad,
            norm_bias_grad,
            second_gain_grad,
            second_bias_grad,
            mix_key_grad,
            mix_gate_grad,
        ]
    )
    square_term = jnp.einsum(
        "prd,pre->pde", square_left, square_right, preferred_element_type=jnp.float32
    )
    square_sum, vector_sum = (
        lax.psum_scatter(square_term, ("batch", "seq"), scatter_dimension=1, tiled=True),
        lax.psum_scatter(vector_term, ("batch", "seq"), scatter_dimension=1, tiled=True),
    )
    return (
        layer_out,
        token_grad,
        square_sum[:5],
        channel_sum[:, :features],
        channel_sum[:, features:],
        square_sum[5],
        vector_sum,
    )


def solution(mesh):
    return jax.shard_map(
        body,
        mesh=mesh,
        in_specs=(
            P("batch", "seq", None),
            P(None, ("batch", "seq"), None),
            P(("batch", "seq"), None),
            P(("batch", "seq"), None),
            P(("batch", "seq"), None),
            P(None, ("batch", "seq")),
            P(),
            P("batch"),
            P("batch", "seq", None),
        ),
        out_specs=(
            P("batch", "seq", None),
            P("batch", "seq", None),
            P(None, ("batch", "seq"), None),
            P(("batch", "seq"), None),
            P(("batch", "seq"), None),
            P(("batch", "seq"), None),
            P(None, ("batch", "seq")),
        ),
        check_vma=False,
    )
```

profile of v0, /device:TPU:1, one launch (start us, length us, event | category | flops | bytes accessed | tf_op | source)
XLA Modules:
  0.0 2861.5 jit_solution(12827458152687937147)
XLA Ops:
  8.8 39.3 %all_gather.35 = bf16[13,2048]{0,1:T(8,128)(2,1)S(1)} all-gather(bf16[13,16]{0,1:T(8,128)(2,1)S(1)} %copy.201), channel_id=1, replica_groups=mesh['batch'=4,'seq'=32] {'batch','seq'}, dimensions={1}, use_global_device_ids=true | all-gather | bytes 53664 | tf_op jit(solution)/shard_map/all_gather | solution.py:122
  57.4 79.7 %all-gather.11.cloned.1.call-done = bf16[5,2048,2048]{2,1,0:T(8,128)(2,1)} async-done(((bf16[5,16,2048]{2,1,0:T(8,128)(2,1)}), bf16[5,2048,2048]{2,1,0:T(8,128)(2,1)}) %all-gather.11.cloned.1.call-update) | async-done | bytes 41943056 | tf_op jit(solution)/shard_map/all_gather | solution.py:121
  137.1 15.0 fusion.4
  152.1 3.1 fusion.103
  158.6 4.0 fusion.48
  164.6 63.6 %all-reduce = f32[1024]{0:T(1024)S(1)} all-reduce(f32[1024]{0:T(1024)S(1)} %get-tuple-element.343), channel_id=2, replica_groups=mesh['batch'=4,'seq'=32] {'seq'}, use_global_device_ids=true, to_apply=%add | all-reduce | flops 1024 | bytes 8192
  238.8 3.0 reshape.841
  244.7 3.3 copy.207
  248.0 3.4 copy.206
  251.4 3.1 multiply_reduce_fusion.4
  259.4 104.1 %all-gather.19.cloned.1.call-done = f32[64,32,64,64]{3,2,1,0:T(8,128)} async-done(((f32[2,32,64,64]{3,2,1,0:T(8,128)}), f32[64,32,64,64]{3,2,1,0:T(8,128)}) %all-gather.19.cloned.1.call-update) | async-done | bytes 33554448 | tf_op jit(solution)/shard_map/all_gather | solution.py:22
  363.5 70.3 %while.30 = (s32[]{:T(128)}, f32[2,32,64,64]{3,2,1,0:T(8,128)S(1)}, s32[]{:T(128)}, f32[32,32]{1,0:T(8,128)S(1)}, f32[32,2,32,64,64]{4,3,2,1,0:T(8,128)}, /*index=5*/s32[]{:T(128)}, s32[]{:T(128)}) while((s32[]{:T(128)}, f32[2,32,64,64]{3,2,1,0:T(8,128)S(1)}, s32[]{:T(128)}, f32[32,32]{1,0:T(8,128)S(1)}, ...), condition=%wide.region_4.5_spmd.clone, body=%wide.region_3.4_spmd.clone.sunk | while | flops 1048580 | bytes 3146225 | solution.py:34
  433.8 7.6 fusion.106
  441.4 12.9 copy.240
  468.3 3.8 multiply_convert_fusion.3
  474.6 3.3 reshape.825
  480.0 5.7 fusion.107
  494.8 15.7 convolution_maximum_fusion
  510.5 57.1 %all-gather.17.cloned.1.call-done = bf16[2048,7168]{1,0:T(8,128)(2,1)} async-done(((bf16[16,7168]{1,0:T(8,128)(2,1)}), bf16[2048,7168]{1,0:T(8,128)(2,1)}) %all-gather.17.cloned.1.call-update) | async-done | bytes 29360144 | tf_op jit(solution)/shard_map/all_gather | solution.py:192
  567.6 16.0 fusion.81
  583.6 56.4 %all-gather.13.cloned.1.call-done = bf16[2048,2048]{1,0:T(8,128)(2,1)} async-done(((bf16[16,2048]{1,0:T(8,128)(2,1)}), bf16[2048,2048]{1,0:T(8,128)(2,1)}) %all-gather.13.cloned.1.call-update) | async-done | bytes 8388624 | tf_op jit(solution)/shard_map/all_gather | solution.py:193
  640.0 7.2 fusion.69
  647.9 14.9 fusion.7
  662.8 16.8 fusion.108
  679.6 7.7 multiply_add_fusion
  704.6 8.4 fusion.100
  715.6 3.0 reshape.831
  720.8 3.3 copy.221
  730.8 62.7 %all-reduce.1 = bf16[1024]{0:T(1024)(128)(2,1)S(1)} all-reduce(bf16[1024]{0:T(1024)(128)(2,1)S(1)} %dynamic-update-slice.1), channel_id=4, replica_groups=mesh['batch'=4,'seq'=32] {'seq'}, use_global_device_ids=true, to_apply=%add.1 | all-reduce | flops 1024 | bytes 4096
  793.6 3.6 fusion.53
  797.2 6.9 copy.228
  807.1 4.2 fusion.43
  814.1 3.3 copy.232
  828.8 3.8 fusion.41
  832.7 9.9 all-gather.21.cloned.1.call-done
  842.6 74.1 %while.31 = (s32[]{:T(128)}, f32[2,32,64,64]{3,2,1,0:T(8,128)S(1)}, s32[]{:T(128)}, bf16[32,32]{1,0:T(8,128)(2,1)S(1)}, bf16[32,2,32,64,64]{4,3,2,1,0:T(8,128)(2...) while((s32[]{:T(128)}, f32[2,32,64,64]{3,2,1,0:T(8,128)S(1)}, s32[]{:T(128)}, ...), condition=%wide.region_14.15_spmd.clone, body=%wide.region_13.14_spmd.clone.sunk | while | flops 1310760 | bytes 2621935 | solution.py:58
  916.8 4.0 fusion.39
  922.1 3.3 copy.239
  928.2 5.3 fusion.29
  933.5 3.4 copy.237
  944.9 17.2 multiply_reduce_fusion
  971.3 37.0 %fusion.14 = f32[6,2048,2048]{2,1,0:T(8,128)} fusion(bf16[6,128,2048]{2,1,0:T(8,128)(2,1)} %copy-done.35, bf16[1,128,2048]{2,1,0:T(8,128)(2,1)} %bitcast.286, bf16[1,128,2048]{2,1,0:T(8,128)(2,1)} %get-tuple-element.320, bf16[4,128,2048]{2,1,0:T(8,128)(2,1)S(1)} %copy-done.32), kind=kOutput, calls=%fused_computation.27 | convolution fusion | flops 6445596672 | bytes 106954752 | tf_op jit(solution)/shard_map/prd,pre->pde/dot_general | solution.py:364
  1008.3 3.7 fusion.80
  1012.0 39.6 %fusion.10 = f32[2,7168,2048]{2,1,0:T(8,128)} fusion(bf16[1,128,7168]{2,1,0:T(8,128)(2,1)} %fusion.80, bf16[1,128,7168]{2,1,0:T(8,128)(2,1)S(1)} %bitcast.268, bf16[1,128,2048]{2,1,0:T(8,128)(2,1)S(1)} %bitcast.285, bf16[1,128,2048]{2,1,0:T(8,128)(2,1)S(1)} %bitcast.275), kind=kOutput, calls=%fused_computation.22 | convolution fusion | flops 7518552064 | bytes 122159104 | tf_op jit(solution)/shard_map/prd,prf->dpf/dot_general | solution.py:227
  1051.6 106.1 %copy.249 = f32[2048,14336]{1,0:T(8,128)} copy(f32[2048,14336]{0,1:T(8,128)} %bitcast.69) | data formatting | bytes 234881024 | tf_op jit(solution)/shard_map/reshape | solution.py:229
  1160.8 441.4 %reduce-scatter.10.cloned.1.call-done = f32[16,13]{1,0:T(8,128)} async-done(((f32[2048,13]{1,0:T(8,128)}), f32[16,13]{1,0:T(8,128)}) %reduce-scatter.10.cloned.1.call-update) | async-done | bytes 848
  1603.5 421.7 %reduce-scatter.6.cloned.1.call-done = f32[6,16,2048]{2,1,0:T(8,128)} async-done(((f32[6,2048,2048]{2,1,0:T(8,128)}), f32[6,16,2048]{2,1,0:T(8,128)}) %reduce-scatter.6.cloned.1.call-update) | async-done | bytes 786448 | tf_op jit(solution)/shard_map/reduce_scatter | solution.py:368
  2028.8 823.7 %reduce-scatter.8.cloned.1.call-done = f32[16,14336]{1,0:T(8,128)} async-done(((f32[2048,14336]{1,0:T(8,128)}), f32[16,14336]{1,0:T(8,128)}) %reduce-scatter.8.cloned.1.call-update) | async-done | bytes 917520 | tf_op jit(solution)/shard_map/reduce_scatter | solution.py:226
  (442 shorter events, 280.9 us)
Async XLA Ops:
  7.2 42.4 %copy-start.18 = (bf16[2,64,2048]{2,1,0:T(8,128)(2,1)S(1)}, bf16[2,64,2048]{2,1,0:T(8,128)(2,1)}, u32[]{:S(2)}) copy-start(bf16[2,64,2048]{2,1,0:T(8,128)(2,1)} %param.13) | copy-start | bytes 1572868
  7.2 46.0 %copy-start.80 = (u32[128]{0:T(128)S(1)}, u32[128]{0:T(128)}, u32[]{:S(2)}) copy-start(u32[128]{0:T(128)} %constant.141) | copy-start | bytes 1540
  7.2 47.3 %copy-start.78 = (f32[32]{0:T(128)S(1)}, f32[32]{0:T(128)}, u32[]{:S(2)}) copy-start(f32[32]{0:T(128)} %param.19) | copy-start | bytes 388
  7.2 129.9 %all-gather.11.cloned.1.call-start = ((), (), s32[]{:S(2)}) async-start(), calls=%async_computation.3 | async-start | bytes 42270720 | tf_op jit(solution)/shard_map/all_gather | solution.py:121
  7.9 355.6 %all-gather.19.cloned.1.call-start = ((), (), s32[]{:S(2)}) async-start(), calls=%async_computation.9 | async-start | bytes 69206016 | tf_op jit(solution)/shard_map/all_gather | solution.py:22
  49.5 6.4 copy-start.60
  49.9 6.1 copy-start.69
  49.9 6.0 copy-start.54
  50.4 4.9 collective-permute-start
  57.4 94.7 %copy-start.31 = (bf16[4,128,2048]{2,1,0:T(8,128)(2,1)}, bf16[4,128,2048]{2,1,0:T(8,128)(2,1)S(1)}, u32[]{:S(2)}) copy-start(bf16[4,128,2048]{2,1,0:T(8,128)(2,1)S(1)} %add_convert_fusion) | copy-start | bytes 6291460
  156.2 6.3 copy-start.10
  162.6 332.2 %all-gather.15.cloned.1.call-start = ((), (), s32[]{:S(2)}) async-start(), calls=%async_computation.5 | async-start | bytes 29589504 | tf_op jit(solution)/shard_map/all_gather | solution.py:191
  163.3 404.3 %all-gather.17.cloned.1.call-start = ((), (), s32[]{:S(2)}) async-start(), calls=%async_computation.6 | async-start | bytes 29589504 | tf_op jit(solution)/shard_map/all_gather | solution.py:192
  163.9 476.1 %all-gather.13.cloned.1.call-start = ((), (), s32[]{:S(2)}) async-start(), calls=%async_computation.4 | async-start | bytes 8454144 | tf_op jit(solution)/shard_map/all_gather | solution.py:193
  164.5 678.2 %all-gather.21.cloned.1.call-start = ((), (), s32[]{:S(2)}) async-start(), calls=%async_computation.10 | async-start | bytes 34603008 | tf_op jit(solution)/shard_map/all_gather | solution.py:40
  363.5 70.3 %copy-start.72 = (f32[32]{0:T(128)S(1)}, f32[32]{0:T(128)}, u32[]{:S(2)}) copy-start(f32[32]{0:T(128)} %get-tuple-element.344) | copy-start | bytes 388
  433.8 7.6 copy-start
  441.4 12.9 copy-start.3
  485.7 5.3 copy-start.77
  488.9 4.4 copy-start.8
  488.9 3.2 collective-permute-start.1
  640.0 7.9 copy-start.2
  662.8 16.8 copy-start.67
  662.8 16.8 copy-start.68
  688.3 11.6 collective-permute-start.2
  704.6 8.4 copy-start.26
  730.5 871.7 %reduce-scatter.10.cloned.1.call-start = ((), (), s32[]{:S(2)}) async-start(), calls=%async_computation.11 | async-start | bytes 1056768
  807.1 4.2 copy-start.1
  807.1 4.2 copy-start.6
  807.1 4.2 copy-start.17
  916.7 4.0 copy-start.7
  916.7 4.0 copy-start.25
  922.1 6.1 copy-start.12
  933.5 6.1 copy-start.34
  944.9 19.6 copy-start.49
  962.1 5.3 copy-start.20
  962.1 5.3 copy-start.55
  962.1 5.3 copy-start.61
  962.2 5.3 copy-start.70
  962.2 5.2 collective-permute-start.3
  964.7 4.8 copy-start.63
  964.7 4.8 copy-start.64
  964.7 4.8 copy-start.65
  964.7 4.8 copy-start.66
  971.0 1054.2 %reduce-scatter.6.cloned.1.call-start = ((), (), s32[]{:S(2)}) async-start(), calls=%async_computation.7 | async-start | bytes 101449728 | tf_op jit(solution)/shard_map/reduce_scatter | solution.py:368
  1008.2 3.8 copy-start.16
  1008.3 3.8 copy-start.33
  1008.3 1844.1 %reduce-scatter.8.cloned.1.call-start = ((), (), s32[]{:S(2)}) async-start(), calls=%async_computation.8 | async-start | bytes 118358016 | tf_op jit(solution)/shard_map/reduce_scatter | solution.py:226
  (46 other events, 100.6 us)
Sparse Core Ops, SparseCore 0:
  11.1 125.9 all-gather.10
  162.7 200.8 all-gather.18
  366.5 98.8 all-gather.14
  468.3 99.3 all-gather.16
  570.4 69.4 all-gather.12
  730.6 111.9 all-gather.20
  971.2 630.9 reduce-scatter.9
  1608.8 416.3 reduce-scatter.5
  2027.8 824.6 reduce-scatter.7
where the time goes:
time: 2880 us; the launch traced here: 2860 us
  waiting for transfers between devices  2000 us (69%)
  matrix products  244 us (8%)
  local copies, waits for them, and re-layouts  241 us (8%)
  other arithmetic  183 us (6%)
  blocking collectives  166 us (6%)
    reduce_scatter x1, waiting for transfers between devices, body(): lax.psum_scatter(jnp.einsum('prd,prf->dpf', channel_left, channel_right,...  824 us
    unnamed x10, waiting for transfers between devices  444 us
    reduce_scatter x1, waiting for transfers between devices, body(): lax.psum_scatter(square_term, ('batch', 'seq'), scatter_dimension=1, tile...  422 us
    unnamed x2, blocking collectives  126 us
    reshape x1, local copies, waits for them, and re-layouts, body(): channel_sum = lax.psum_scatter(jnp.einsum('prd,prf->dpf', channel_left, c...  106 us
    all_gather x1, waiting for transfers between devices, carried_in(): everything = jax.tree.map(lambda part: lax.all_gather(part, axis), array)  104 us
    all_gather x1, waiting for transfers between devices, body(): lax.all_gather(time_weights, ('batch', 'seq'), axis=1, tiled=True)  79.7 us
    select_n x32, other arithmetic, entering_lap(): return jax.tree.map(lambda a, b: jnp.where(reached, a, b), new, before)  72.3 us
  transfers between devices with their start and end apart: 13, of which 9 were waited for; matrix products, arithmetic and copies ran while one was open for 15% of the time, Pallas kernels for 0%

commit v1 on v0

v1 whole, which is shorter than its diff:
```python
import jax
import jax.numpy as jnp
from jax import lax
from jax.experimental import pallas as pl
from jax.experimental.pallas import tpu as pltpu
from jax.sharding import Mesh, PartitionSpec as P

BLOCK_LEN = 64
epsilon = 1e-05
group_epsilon = 0.00064

GROUP = ("y", "core")
ROWS = ("z", "x")
SEQ = ("x", "y", "core")
ALL = ("z", "x", "y", "core")
low = jnp.bfloat16


MESH = pl.DeviceIdType.MESH
HBM = pl.BlockSpec(memory_space=pl.ANY)
VMEM = pl.BlockSpec(memory_space=pltpu.VMEM)


def greet(devices):
    barrier = pltpu.get_barrier_semaphore()
    for device in devices:
        pl.semaphore_signal(barrier, inc=1, device_id=device, device_id_type=MESH)
    pl.semaphore_wait(barrier, len(devices))

def ring_places():
    y, c = lax.axis_index("y"), lax.axis_index("core")
    right, left, far = lax.rem(y + 1, 4), lax.rem(y + 3, 4), lax.rem(y + 2, 4)
    return y, c, right, left, far

def gather_kernel(x_ref, out_ref, send, recv, local):
    y, c, right, left, far = ring_places()
    to_sibling, to_right, to_left = {"core": 1 - c}, {"y": right}, {"y": left}
    greet([to_sibling, to_right, to_left])
    rows = x_ref.shape[0]
    half = rows // 2
    first, last = pl.ds(0, half), pl.ds(half, half)
    def copy(k, src, dst, device):
        return pltpu.make_async_remote_copy(src_ref=src, dst_ref=dst, send_sem=send.at[k], recv_sem=recv.at[k], device_id=device, device_id_type=MESH)
    slot = lambda place: out_ref.at[place * 2 + c]
    own = pltpu.make_async_copy(x_ref, slot(y), local)
    right_1 = copy(0, x_ref.at[first], slot(y).at[first], to_right)
    left_1 = copy(1, x_ref.at[last], slot(y).at[last], to_left)
    right_2 = copy(2, x_ref.at[last], slot(y).at[last], to_right)
    left_2 = copy(3, x_ref.at[first], slot(y).at[first], to_left)
    near = copy(4, x_ref, slot(y), to_sibling)
    for one in (right_1, left_1, right_2, left_2, near):
        one.start()
    own.start()
    right_1.wait_recv()
    far_right = copy(5, slot(left).at[first], slot(left).at[first], to_right)
    far_right.start()
    left_1.wait_recv()
    far_left = copy(6, slot(right).at[last], slot(right).at[last], to_left)
    far_left.start()
    right_2.wait_recv()
    pass_left = copy(7, slot(left), slot(left), to_sibling)
    pass_left.start()
    left_2.wait_recv()
    pass_right = copy(8, slot(right), slot(right), to_sibling)
    pass_right.start()
    far_right.wait_recv()
    pass_first = copy(9, slot(far).at[first], slot(far).at[first], to_sibling)
    pass_first.start()
    far_left.wait_recv()
    pass_last = copy(10, slot(far).at[last], slot(far).at[last], to_sibling)
    pass_last.start()
    for one in (near, pass_left, pass_right, pass_first, pass_last):
        one.wait_recv()
    for one in (right_1, left_1, right_2, left_2, near, far_right, far_left, pass_left, pass_right, pass_first, pass_last):
        one.wait_send()
    own.wait()

def gather(x, cid):
    return pl.pallas_call(
        gather_kernel,
        out_shape=jax.ShapeDtypeStruct((8,) + x.shape, x.dtype),
        in_specs=[HBM], out_specs=HBM,
        scratch_shapes=[pltpu.SemaphoreType.DMA((11,)), pltpu.SemaphoreType.DMA((11,)), pltpu.SemaphoreType.DMA],
        compiler_params=pltpu.CompilerParams(collective_id=cid, has_side_effects=True),
    )(x)

def scatter_kernel(p_ref, out_ref, from_sibling, mid, from_left, from_right, end_left, end_right, send, recv):
    y, c, right, left, far = ring_places()
    to_sibling, to_right, to_left = {"core": 1 - c}, {"y": right}, {"y": left}
    greet([to_sibling, to_right, to_left])
    half = p_ref.shape[1] // 2
    first, last = pl.ds(0, half), pl.ds(half, half)
    def copy(k, src, dst, device):
        return pltpu.make_async_remote_copy(src_ref=src, dst_ref=dst, send_sem=send.at[k], recv_sem=recv.at[k], device_id=device, device_id_type=MESH)
    order = (far, right, left, y)
    near = [copy(k, p_ref.at[order[k] * 2 + 1 - c], from_sibling.at[k], to_sibling) for k in range(4)]
    for one in near:
        one.start()
    def summed(k, rows):
        return p_ref[order[k] * 2 + c, rows].astype(jnp.float32) + from_sibling[k, rows].astype(jnp.float32)
    near[0].wait_recv()
    mid[0] = summed(0, slice(None)).astype(low)
    far_right = copy(4, mid.at[0, first], from_left, to_right)
    far_left = copy(5, mid.at[0, last], from_right, to_left)
    far_right.start(); far_left.start()
    near[1].wait_recv()
    mid[1, last] = summed(1, last).astype(low)
    right_b = copy(6, mid.at[1, last], end_left.at[last], to_right)
    right_b.start()
    near[2].wait_recv()
    mid[2, first] = summed(2, first).astype(low)
    left_b = copy(7, mid.at[2, first], end_right.at[first], to_left)
    left_b.start()
    far_right.wait_recv()
    mid[1, first] = (summed(1, first) + from_left[...].astype(jnp.float32)).astype(low)
    right_a = copy(8, mid.at[1, first], end_left.at[first], to_right)
    right_a.start()
    far_left.wait_recv()
    mid[2, last] = (summed(2, last) + from_right[...].astype(jnp.float32)).astype(low)
    left_a = copy(9, mid.at[2, last], end_right.at[last], to_left)
    left_a.start()
    near[3].wait_recv()
    out_ref[...] = summed(3, slice(None))
    right_b.wait_recv()
    out_ref[last] += end_left[last].astype(jnp.float32)
    left_b.wait_recv()
    out_ref[first] += end_right[first].astype(jnp.float32)
    right_a.wait_recv()
    out_ref[first] += end_left[first].astype(jnp.float32)
    left_a.wait_recv()
    out_ref[last] += end_right[last].astype(jnp.float32)
    for one in near + [far_right, far_left, right_b, left_b, right_a, left_a]:
        one.wait_send()

def scatter(p, cid):
    _, rows, cols = p.shape
    return pl.pallas_call(
        scatter_kernel,
        out_shape=jax.ShapeDtypeStruct((rows, cols), jnp.float32),
        in_specs=[VMEM], out_specs=VMEM,
        scratch_shapes=[pltpu.VMEM((4, rows, cols), low), pltpu.VMEM((3, rows, cols), low), pltpu.VMEM((rows // 2, cols), low), pltpu.VMEM((rows // 2, cols), low),
            pltpu.VMEM((rows, cols), low), pltpu.VMEM((rows, cols), low), pltpu.SemaphoreType.DMA((10,)), pltpu.SemaphoreType.DMA((10,))],
        compiler_params=pltpu.CompilerParams(collective_id=cid, has_side_effects=True, vmem_limit_bytes=40 * 2**20),
    )(p)

def exchange_kernel(x_ref, out_ref, send, recv, local):
    y, c = lax.axis_index("y"), lax.axis_index("core")
    me = y * 2 + c
    places = [lax.rem(me + k, 8) for k in range(1, 8)]
    devices = [{"y": p // 2, "core": lax.rem(p, 2)} for p in places]
    greet(devices)
    copies = [pltpu.make_async_remote_copy(src_ref=x_ref.at[p], dst_ref=out_ref.at[me], send_sem=send.at[k], recv_sem=recv.at[k], device_id=d, device_id_type=MESH)
        for k, (p, d) in enumerate(zip(places, devices))]
    for k in (3, 2, 4, 1, 5, 0, 6):
        copies[k].start()
    own = pltpu.make_async_copy(x_ref.at[me], out_ref.at[me], local)
    own.start()
    for one in copies:
        one.wait()
    own.wait()

def exchange(x, cid):
    return pl.pallas_call(
        exchange_kernel,
        out_shape=jax.ShapeDtypeStruct(x.shape, x.dtype),
        in_specs=[HBM], out_specs=HBM,
        scratch_shapes=[pltpu.SemaphoreType.DMA((7,)), pltpu.SemaphoreType.DMA((7,)), pltpu.SemaphoreType.DMA],
        compiler_params=pltpu.CompilerParams(collective_id=cid, has_side_effects=True),
    )(x)

def line_kernel(x_ref, out_ref, send, recv, local):
    me = lax.axis_index("x")
    devices = [{"x": lax.rem(me + k, 4)} for k in range(1, 4)]
    greet(devices)
    copies = [pltpu.make_async_remote_copy(src_ref=x_ref, dst_ref=out_ref.at[me], send_sem=send.at[k], recv_sem=recv.at[k], device_id=d, device_id_type=MESH)
        for k, d in enumerate(devices)]
    for k in (1, 0, 2):
        copies[k].start()
    own = pltpu.make_async_copy(x_ref, out_ref.at[me], local)
    own.start()
    for one in copies:
        one.wait()
    own.wait()

def line(x, cid):
    return pl.pallas_call(
        line_kernel,
        out_shape=jax.ShapeDtypeStruct((4,) + x.shape, x.dtype),
        in_specs=[HBM], out_specs=HBM,
        scratch_shapes=[pltpu.SemaphoreType.DMA((3,)), pltpu.SemaphoreType.DMA((3,)), pltpu.SemaphoreType.DMA],
        compiler_params=pltpu.CompilerParams(collective_id=cid, has_side_effects=True),
    )(x)

def cube_places():
    z, x, y, c = [lax.axis_index(name) for name in ("z", "x", "y", "core")]
    place, member = z * 4 + x, y * 2 + c
    far = [lax.rem(place + k, 16) for k in range(1, 16)]
    near = [lax.rem(member + k, 8) for k in range(1, 8)]
    return place, member, far, near, [{"z": p // 4, "x": lax.rem(p, 4)} for p in far], [{"y": p // 2, "core": lax.rem(p, 2)} for p in near]

def settings_kernel(x_ref, out_ref, blocks, stripe, send, recv):
    place, member, far, near, far_devices, near_devices = cube_places()
    greet(far_devices + near_devices)
    first = [pltpu.make_async_remote_copy(src_ref=x_ref, dst_ref=blocks.at[k], send_sem=send.at[k], recv_sem=recv.at[k], device_id=d, device_id_type=MESH) for k, d in enumerate(near_devices)]
    for one in first:
        one.start()
    total = x_ref[...].astype(jnp.float32)
    for k, one in enumerate(first):
        one.wait_recv()
        total = total + blocks[k].astype(jnp.float32)
    stripe[...] = total.astype(low)
    second = [pltpu.make_async_remote_copy(src_ref=stripe, dst_ref=out_ref.at[place], send_sem=send.at[7 + k], recv_sem=recv.at[7 + k], device_id=d, device_id_type=MESH) for k, d in enumerate(far_devices)]
    for one in second:
        one.start()
    out_ref[place] = stripe[...]
    for one in second:
        one.wait()
    for one in first:
        one.wait_send()

def gather_settings(x, cid):
    return pl.pallas_call(
        settings_kernel,
        out_shape=jax.ShapeDtypeStruct((16, 16, 128), low),
        in_specs=[VMEM], out_specs=VMEM,
        scratch_shapes=[pltpu.VMEM((7, 16, 128), low), pltpu.VMEM((16, 128), low), pltpu.SemaphoreType.DMA((22,)), pltpu.SemaphoreType.DMA((22,))],
        compiler_params=pltpu.CompilerParams(collective_id=cid, has_side_effects=True),
    )(x)

def total_kernel(x_ref, out_ref, far_blocks, near_blocks, stripe, send, recv):
    place, member, far, near, far_devices, near_devices = cube_places()
    greet(far_devices + near_devices)
    first = [pltpu.make_async_remote_copy(src_ref=x_ref.at[p], dst_ref=far_blocks.at[k], send_sem=send.at[7 + k], recv_sem=recv.at[7 + k], device_id=d, device_id_type=MESH) for k, (p, d) in enumerate(zip(far, far_devices))]
    for one in first:
        one.start()
    total = x_ref[place]
    for k, one in enumerate(first):
        one.wait_recv()
        total = total + far_blocks[k]
    stripe[...] = total
    second = [pltpu.make_async_remote_copy(src_ref=stripe, dst_ref=near_blocks.at[k], send_sem=send.at[k], recv_sem=recv.at[k], device_id=d, device_id_type=MESH) for k, d in enumerate(near_devices)]
    for one in second:
        one.start()
    for k, one in enumerate(second):
        one.wait_recv()
        total = total + near_blocks[k]
    out_ref[...] = total
    for one in first + second:
        one.wait_send()

def total_vectors(x, cid):
    return pl.pallas_call(
        total_kernel,
        out_shape=jax.ShapeDtypeStruct((16, 128), jnp.float32),
        in_specs=[VMEM], out_specs=VMEM,
        scratch_shapes=[pltpu.VMEM((15, 16, 128), jnp.float32), pltpu.VMEM((7, 16, 128), jnp.float32), pltpu.VMEM((16, 128), jnp.float32), pltpu.SemaphoreType.DMA((22,)), pltpu.SemaphoreType.DMA((22,))],
        compiler_params=pltpu.CompilerParams(collective_id=cid, has_side_effects=True),
    )(x)


def shifted(block, axis, distance):
    devices = range(lax.axis_size(axis))
    route = [(i - distance, i) for i in devices if i - distance in devices]
    return lax.ppermute(block, axis, route)


def layer_norm(values, gain_row, offset):
    center = values - jnp.mean(values, axis=-1, keepdims=True)
    inverse = lax.rsqrt(jnp.mean(center * center, axis=-1, keepdims=True) + epsilon)
    scaled = center * inverse
    return (scaled * gain_row + offset, scaled, inverse)


def norm_back(upstream, scaled, inverse, gain_row):
    inner_grad = upstream * gain_row
    return inverse * (
        inner_grad
        - jnp.mean(inner_grad, axis=-1, keepdims=True)
        - scaled * jnp.mean(inner_grad * scaled, axis=-1, keepdims=True)
    )


def dot_to(left, right):
    return jnp.dot(left, right, preferred_element_type=jnp.float32)


def dot_right(left, right):
    return lax.dot_general(left, right, (((1,), (1,)), ((), ())), preferred_element_type=jnp.float32)


def dot_left(left, right):
    return lax.dot_general(left, right, (((0,), (0,)), ((), ())), preferred_element_type=jnp.float32)


def mul(spec, left, right):
    return jnp.einsum(spec, left.astype(low), right.astype(low), preferred_element_type=jnp.float32)


def body(tokens, time_weights, channel_key, channel_value, channel_gate, vectors, head_decay, lengths, cotangent):
    groups, span, width = tokens.shape
    features = channel_key.shape[1]
    local_rows = channel_key.shape[0]
    members = lax.axis_size(GROUP)
    member = lax.axis_index(GROUP)
    x_size, x_place = lax.axis_size("x"), lax.axis_index("x")
    heads = head_decay.shape[0] // members
    head_width = width // head_decay.shape[0]
    own = width // members
    own_features = features // members
    row_count = groups * span
    all_rows = members * row_count
    stripe = members * local_rows

    time_part = jnp.swapaxes(time_weights, 0, 1).reshape(local_rows, 5, members, own)
    time_part = lax.all_to_all(time_part, GROUP, split_axis=2, concat_axis=0, tiled=True)
    time_full = lax.all_gather(time_part.reshape(stripe, 5 * own), ROWS, axis=0, tiled=True)
    channel_part = jnp.concatenate(
        [
            channel_key.reshape(local_rows, members, own_features),
            channel_value.reshape(local_rows, members, own_features),
            channel_gate.reshape(local_rows, members, own),
        ],
        axis=2,
    )
    channel_part = lax.all_to_all(channel_part, GROUP, split_axis=1, concat_axis=0, tiled=True)
    channel_part = channel_part.reshape(stripe, 2 * own_features + own)
    channel_part, time_full = lax.optimization_barrier((channel_part, time_full))
    channel_full = lax.all_gather(channel_part, ROWS, axis=0, tiled=True)
    key_full, value_full = channel_full[:, :own_features], channel_full[:, own_features : 2 * own_features]
    gate_full = channel_full[:, 2 * own_features :]
    out_full = time_full[:, 4 * own :].reshape(members, own, own)
    vector_rows = vectors.shape[0]
    vector_block = lax.dynamic_update_slice(
        jnp.zeros((16, stripe), low), vectors, (0, member * local_rows)
    )
    vector_full = jnp.swapaxes(gather_settings(vector_block, 1), 0, 1).reshape(16, width)[:vector_rows]
    settings = vector_full.astype(jnp.float32)
    own_settings = lax.dynamic_slice_in_dim(settings, member * own, own, axis=1)

    inputs_all = gather(tokens.reshape(row_count, width), 2).reshape(members, groups, span, width)
    first_norm, first_scaled, _ = layer_norm(inputs_all.astype(jnp.float32), settings[0], settings[1])
    edge_norm, _, _ = layer_norm(shifted(inputs_all[-1, :, -1, :], "x", 1).astype(jnp.float32), settings[0], settings[1])
    edge_norm = jnp.where(x_place > 0, edge_norm, 0.0)
    before = jnp.concatenate([edge_norm[None], first_norm[:-1, :, -1, :]], axis=0)
    first_prev = jnp.concatenate([before[:, :, None, :], first_norm[:, :, :-1, :]], axis=2)
    first_delta = (first_norm - first_prev).reshape(all_rows, width)
    first_prev = first_prev.reshape(all_rows, width)
    mix_low = [(first_prev + settings[2 + p] * first_delta).astype(low) for p in range(4)]
    projected = [dot_to(mix_low[p], time_full[:, p * own : (p + 1) * own]) for p in range(4)]
    gate_pre = projected[3]
    gate_act = jax.nn.silu(gate_pre)

    log_decay = jnp.log(lax.dynamic_slice_in_dim(head_decay, member * heads, heads))
    places = jnp.arange(BLOCK_LEN, dtype=jnp.float32)
    below = places[:, None] > places[None, :]
    spread = jnp.where(below, places[:, None] - 1.0 - places[None, :], 0.0)
    mask_table = jnp.where(below[None], jnp.exp(spread[None] * log_decay[:, None, None]), 0.0)
    enter_decay = jnp.exp(places[:, None] * log_decay[None, :])
    leave_decay = jnp.exp((BLOCK_LEN - 1.0 - places)[:, None] * log_decay[None, :])
    block_decay = jnp.exp(BLOCK_LEN * log_decay)[None, :, None, None]

    def power(count):
        return jnp.exp(count * log_decay)[None, :, None, None]

    identity = jnp.eye(BLOCK_LEN, dtype=jnp.float32)
    block_shape = (members, groups, BLOCK_LEN, heads, head_width)
    recv, key, value = [projected[p].astype(low).reshape(block_shape) for p in range(3)]
    bonus = own_settings[6].reshape(heads, head_width)
    recv_wide, key_wide = recv.astype(jnp.float32), key.astype(jnp.float32)
    scores = mul("msihe,msjhe->mshij", recv, key)
    self_pair = jnp.sum(recv_wide * bonus * key_wide, axis=-1)
    weights = (scores * mask_table + identity * jnp.swapaxes(self_pair, 2, 3)[..., None]).astype(low)
    intra = mul("mshij,msjhe->msihe", weights, value)
    key_leave = (key_wide * leave_decay[:, :, None]).astype(low)
    block_states = mul("msjhe,msjhf->mshef", key_leave, value)
    running = jnp.zeros_like(block_states[0])
    prefixes = []
    for m in range(members):
        prefixes.append(running)
        running = running * block_decay + block_states[m]
    every_state = line(running.reshape(-1, 128), 3).reshape((x_size,) + running.shape)
    entering = jnp.zeros_like(running)
    span_decay = power(float(BLOCK_LEN * members))
    for x in range(x_size - 1):
        entering = jnp.where(x < x_place, entering * span_decay + every_state[x], entering)
    incoming = jnp.stack([prefixes[m] + power(float(BLOCK_LEN * m)) * entering for m in range(members)])
    incoming = incoming.astype(low)
    recv_enter = (recv_wide * enter_decay[:, :, None]).astype(low)
    wkv = (intra + mul("msihe,mshef->msihf", recv_enter, incoming)).reshape(all_rows, heads, head_width)
    wkv_center = wkv - jnp.mean(wkv, axis=-1, keepdims=True)
    wkv_inverse = lax.rsqrt(jnp.mean(wkv_center * wkv_center, axis=-1, keepdims=True) + group_epsilon)
    wkv_scaled = wkv_center * wkv_inverse
    normed = wkv_scaled.reshape(all_rows, own) * own_settings[7] + own_settings[8]
    gated_own = (normed * gate_act).astype(low)
    gated_all = gather(gated_own, 5)
    out_own = jnp.einsum("mre,med->rd", gated_all, out_full, preferred_element_type=jnp.float32)
    out = exchange(out_own.astype(low).reshape(members, row_count, own), 6)

    inputs = tokens.astype(jnp.float32)
    hidden_one = inputs.reshape(row_count, width) + jnp.swapaxes(out, 0, 1).reshape(row_count, width).astype(jnp.float32)
    second, second_scaled, second_inverse = layer_norm(
        hidden_one.reshape(groups, span, width), settings[9], settings[10]
    )
    second_all = gather(second.astype(low).reshape(row_count, width), 7).reshape(members, groups, span, width)
    second_edge = shifted(second_all[-1, :, -1, :], "x", 1)
    before = jnp.concatenate([second_edge[None], second_all[:-1, :, -1, :]], axis=0)
    second_prev = jnp.concatenate([before[:, :, None, :], second_all[:, :, :-1, :]], axis=2)
    second_prev = second_prev.reshape(all_rows, width).astype(jnp.float32)
    second_delta = second_all.reshape(all_rows, width).astype(jnp.float32) - second_prev
    ckey = (second_prev + settings[11] * second_delta).astype(low)
    cgate = (second_prev + settings[12] * second_delta).astype(low)
    rectified = jax.nn.relu(dot_to(ckey, key_full))
    hidden = (rectified * rectified).astype(low)
    value_out = scatter(dot_right(hidden, value_full).astype(low).reshape(members, row_count, width), 8)
    gate_pre_own = dot_to(cgate, gate_full).astype(low).reshape(members, row_count, own)
    channel_pre = jnp.swapaxes(exchange(gate_pre_own, 9), 0, 1).reshape(row_count, width)
    gate_sig = jax.nn.sigmoid(channel_pre.astype(jnp.float32))
    layer_out = (hidden_one + gate_sig * value_out).reshape(groups, span, width).astype(low)

    seq_place = lax.axis_index(SEQ)
    offsets = seq_place * span + jnp.arange(span, dtype=jnp.int32)
    valid = (offsets[None, :] < lengths[:, None]).astype(jnp.float32)
    upstream = (cotangent.astype(jnp.float32) * valid[:, :, None]).reshape(row_count, width)
    grad_value = (upstream * gate_sig).astype(low)
    grad_gate = (upstream * value_out * gate_sig * (1.0 - gate_sig)).astype(low)
    grad_value_all = gather(grad_value, 10).reshape(all_rows, width)
    grad_gate_own = exchange(jnp.swapaxes(grad_gate.reshape(row_count, members, own), 0, 1), 11).reshape(all_rows, own)
    grad_key = (2.0 * dot_to(grad_value_all, value_full) * rectified).astype(low)
    grad_ckey = dot_right(grad_key, key_full)
    grad_cgate = dot_right(grad_gate_own, gate_full)
    mix_key_grad = jnp.sum(second_delta * grad_ckey, axis=0)
    mix_gate_grad = jnp.sum(second_delta * grad_cgate, axis=0)
    grad_second = (settings[11] * grad_ckey + settings[12] * grad_cgate).reshape(members, groups, span, width)
    grad_prev = ((1.0 - settings[11]) * grad_ckey + (1.0 - settings[12]) * grad_cgate).reshape(
        members, groups, span, width
    )
    second_back = shifted(grad_prev[0, :, 0, :], "x", -1)
    after = jnp.concatenate([grad_prev[1:, :, 0, :], second_back[None]], axis=0)
    grad_second = grad_second + jnp.concatenate([grad_prev[:, :, 1:, :], after[:, :, None, :]], axis=2)
    grad_second = scatter(grad_second.astype(low).reshape(members, row_count, width), 8).reshape(groups, span, width)
    channel_term = jnp.concatenate(
        [
            dot_left(ckey, grad_key).astype(low),
            dot_left(grad_value_all, hidden).astype(low),
            dot_left(cgate, grad_gate_own).astype(low),
        ],
        axis=1,
    )
    channel_term, grad_second = lax.optimization_barrier((channel_term, grad_second))
    channel_sum = lax.psum_scatter(channel_term, ROWS, scatter_dimension=0, tiled=True)
    channel_sum = lax.all_to_all(
        channel_sum.reshape(members, local_rows, 2 * own_features + own), GROUP, split_axis=0, concat_axis=0, tiled=True
    )
    channel_sum = jnp.swapaxes(channel_sum, 0, 1).astype(jnp.float32)
    key_grad = channel_sum[:, :, :own_features].reshape(local_rows, features)
    value_grad = channel_sum[:, :, own_features : 2 * own_features].reshape(local_rows, features)
    gate_grad = channel_sum[:, :, 2 * own_features :].reshape(local_rows, width)
    second_gain_grad = jnp.sum(grad_second * second_scaled, axis=(0, 1))
    second_bias_grad = jnp.sum(grad_second, axis=(0, 1))
    grad_hidden_one = upstream + norm_back(grad_second, second_scaled, second_inverse, settings[9]).reshape(
        row_count, width
    )
    grad_out = grad_hidden_one.astype(low)
    grad_out_own = exchange(jnp.swapaxes(grad_out.reshape(row_count, members, own), 0, 1), 12).reshape(all_rows, own)
    grad_gated = scatter(
        jnp.einsum("rd,med->mre", grad_out_own, out_full, preferred_element_type=jnp.float32).astype(low), 13
    )
    out_term = jnp.einsum("mre,rd->med", gated_all, grad_out_own, preferred_element_type=jnp.float32).astype(low)
    grad_normed = grad_gated * gate_act
    gate_sigma = jax.nn.sigmoid(gate_pre)
    grad_gate_pre = (grad_gated * normed * gate_sigma * (1.0 + gate_pre * (1.0 - gate_sigma))).astype(low)
    norm_gain_grad = jnp.sum(grad_normed * wkv_scaled.reshape(all_rows, own), axis=0)
    norm_bias_grad = jnp.sum(grad_normed, axis=0)
    grad_wkv = norm_back(
        grad_normed.reshape(all_rows, heads, head_width),
        wkv_scaled,
        wkv_inverse,
        own_settings[7].reshape(heads, head_width),
    )
    grad_wkv = grad_wkv.astype(low).reshape(block_shape)
    grad_weights = mul("msihf,msjhf->mshij", grad_wkv, value).astype(low).astype(jnp.float32)
    masked = (grad_weights * mask_table).astype(low)
    self_back = jnp.swapaxes(jnp.sum(grad_weights * identity, axis=4), 2, 3)[..., None]
    bonus_grad = jnp.sum(self_back * recv_wide * key_wide, axis=(0, 1, 2)).reshape(own)
    grad_incoming = mul("msihe,msihf->mshef", recv_enter, grad_wkv)
    running = jnp.zeros_like(grad_incoming[0])
    suffixes = []
    for m in reversed(range(members)):
        suffixes.append(running)
        running = running * block_decay + grad_incoming[m]
    every_grad = line(running.reshape(-1, 128), 4).reshape((x_size,) + running.shape)
    leaving = jnp.zeros_like(running)
    for x in reversed(range(1, x_size)):
        leaving = jnp.where(x > x_place, leaving * span_decay + every_grad[x], leaving)
    grad_states = jnp.stack(
        [suffixes[members - 1 - m] + power(float(BLOCK_LEN * (members - 1 - m))) * leaving for m in range(members)]
    ).astype(low)
    grad_recv = (
        mul("mshij,msjhe->msihe", masked, key)
        + self_back * bonus * key_wide
        + mul("msihf,mshef->msihe", grad_wkv, incoming) * enter_decay[:, :, None]
    )
    grad_lookup = (
        mul("mshij,msihe->msjhe", masked, recv)
        + self_back * bonus * recv_wide
        + mul("msjhf,mshef->msjhe", value, grad_states) * leave_decay[:, :, None]
    )
    grad_values = mul("mshij,msihf->msjhf", weights, grad_wkv) + mul("msjhe,mshef->msjhf", key_leave, grad_states)
    grad_proj = [
        grad_recv.reshape(all_rows, own).astype(low),
        grad_lookup.reshape(all_rows, own).astype(low),
        grad_values.reshape(all_rows, own).astype(low),
        grad_gate_pre,
    ]
    time_term = jnp.concatenate(
        [dot_left(mix_low[p], grad_proj[p]).astype(low) for p in range(4)] + [out_term.reshape(width, own)], axis=1
    )
    time_sum = lax.psum_scatter(time_term, ROWS, scatter_dimension=0, tiled=True)
    time_sum = lax.all_to_all(
        time_sum.reshape(members, local_rows, 5, own), GROUP, split_axis=0, concat_axis=0, tiled=True
    ).astype(jnp.float32)
    time_grads = jnp.transpose(time_sum, (2, 1, 0, 3)).reshape(5, local_rows, width)
    grad_mix = [dot_right(grad_proj[p], time_full[:, p * own : (p + 1) * own]) for p in range(4)]
    mix_grads = [jnp.sum(first_delta * grad_mix[p], axis=0) for p in range(4)]
    grad_first = sum(settings[2 + p] * grad_mix[p] for p in range(4)).reshape(members, groups, span, width)
    grad_prev = sum((1.0 - settings[2 + p]) * grad_mix[p] for p in range(4)).reshape(members, groups, span, width)
    first_back = shifted(grad_prev[0, :, 0, :], "x", -1)
    after = jnp.concatenate([grad_prev[1:, :, 0, :], first_back[None]], axis=0)
    grad_first = grad_first + jnp.concatenate([grad_prev[:, :, 1:, :], after[:, :, None, :]], axis=2)
    grad_first = scatter(grad_first.astype(low).reshape(members, row_count, width), 8).reshape(groups, span, width)
    own_center = inputs - jnp.mean(inputs, axis=-1, keepdims=True)
    own_inverse = lax.rsqrt(jnp.mean(own_center * own_center, axis=-1, keepdims=True) + epsilon)
    own_scaled = own_center * own_inverse
    first_gain_grad = jnp.sum(grad_first * own_scaled, axis=(0, 1))
    first_bias_grad = jnp.sum(grad_first, axis=(0, 1))
    token_grad = (
        grad_hidden_one.reshape(groups, span, width) + norm_back(grad_first, own_scaled, own_inverse, settings[0])
    ).astype(low)

    def spread_own(row):
        return lax.dynamic_update_slice_in_dim(jnp.zeros((width,), jnp.float32), row, member * own, axis=0)

    vector_term = jnp.stack(
        [
            first_gain_grad,
            first_bias_grad,
            *mix_grads,
            spread_own(bonus_grad),
            spread_own(norm_gain_grad),
            spread_own(norm_bias_grad),
            second_gain_grad,
            second_bias_grad,
            mix_key_grad,
            mix_gate_grad,
        ]
    )
    vector_term = jnp.pad(vector_term, ((0, 16 - vector_rows), (0, 0))).reshape(16, width // stripe, stripe)
    vector_sum = total_vectors(jnp.swapaxes(vector_term, 0, 1), 14)
    vector_sum = lax.dynamic_slice(vector_sum, (0, member * local_rows), (vector_rows, local_rows))
    return layer_out, token_grad, time_grads, key_grad, value_grad, gate_grad, vector_sum


def solution(mesh):
    batch, seq = mesh.devices.shape
    side = 4
    fine = Mesh(mesh.devices.reshape(batch, side, seq // (2 * side), 2), ALL)
    return jax.shard_map(
        body,
        mesh=fine,
        in_specs=(
            P("z", SEQ, None),
            P(None, ALL, None),
            P(ALL, None),
            P(ALL, None),
            P(ALL, None),
            P(None, ALL),
            P(),
            P("z"),
            P("z", SEQ, None),
        ),
        out_specs=(
            P("z", SEQ, None),
            P("z", SEQ, None),
            P(None, ALL, None),
            P(ALL, None),
            P(ALL, None),
            P(ALL, None),
            P(None, ALL),
        ),
        check_vma=False,
    )
```

time: 2880 us -> 831 us (0.29)
  waiting for transfers between devices: 2000 us -> 41 us
  Pallas kernels: 0 us -> 284 us
  blocking collectives: 166 us -> 13.4 us
  local copies, waits for them, and re-layouts: 241 us -> 154 us
  matrix products: 244 us -> 160 us
  other arithmetic: 183 us -> 133 us
    reduce_scatter x2, waiting for transfers between devices: 1250 us -> 36.9 us  [the longest x1 36.9 us: body(): lax.psum_scatter(channel_term, ROWS, scatter_dimension=0, tiled=True)]
    unnamed x10 -> x4, waiting for transfers between devices: 444 us -> 0.07 us
    all_gather x6 -> x2, waiting for transfers between devices: 307 us -> 0.01 us  [the longest x1 0.01 us: body(): lax.all_gather(time_part.reshape(stripe, 5 * own), ROWS, axis=0, tiled=True)]
    pallas_call x0 -> x16, Pallas kernels: none -> 284 us  [the longest x4 94.2 us: gather(): pl.pallas_call(gather_kernel, out_shape=jax.ShapeDtypeStruct((8,) + x.sha...]
    select_n x65 -> x1, other arithmetic: 143 us -> 0.1 us  [body(): jnp.where(below[None], jnp.exp(spread[None] * log_decay[:, None, None]),...]
    unnamed x2 -> x0, blocking collectives: 126 us -> none
    reshape x6 -> x18, local copies, waits for them, and re-layouts: 121 us -> 28.1 us  [the longest x2 7.3 us: body(): (intra + mul('msihe,mshef->msihf', recv_enter, incoming)).reshape(all_row...]
    dot_general x24 -> x36, matrix products: 244 us -> 160 us  [the longest x7 66.5 us: dot_right(): lax.dot_general(left, right, (((1,), (1,)), ((), ())), preferred_element_...]
  transfers between devices with their start and end apart: 13 -> 11, of which waited for: 9 -> 2; matrix products, arithmetic and copies ran while one was open for 15% -> 30% of each run, Pallas kernels for 0% -> 18%
where the time goes in v1:
time: 831 us; the launch traced here: 823 us
  Pallas kernels  284 us (34%)
  matrix products  160 us (19%)
  local copies, waits for them, and re-layouts  154 us (19%)
  other arithmetic  133 us (16%)
  waiting for transfers between devices  41 us (5%)
  starting transfers between devices  21.4 us (3%)
  between operations  16.6 us (2%)
  blocking collectives  13.4 us (2%)
    pallas_call x4, Pallas kernels, gather(): pl.pallas_call(gather_kernel, out_shape=jax.ShapeDtypeStruct((8,) + x.sha...  94.2 us
    pallas_call x4, Pallas kernels, scatter(): pl.pallas_call(scatter_kernel, out_shape=jax.ShapeDtypeStruct((rows, cols...  92.6 us
    dot_general x7, matrix products, dot_right(): lax.dot_general(left, right, (((1,), (1,)), ((), ())), preferred_element_...  66.5 us
    pallas_call x4, Pallas kernels, exchange(): pl.pallas_call(exchange_kernel, out_shape=jax.ShapeDtypeStruct(x.shape, x...  39.2 us
    dot_general x7, matrix products, dot_to(): return jnp.dot(left, right, preferred_element_type=jnp.float32)  37.2 us
    reduce_scatter x1, waiting for transfers between devices, body(): lax.psum_scatter(channel_term, ROWS, scatter_dimension=0, tiled=True)  36.9 us
    unnamed x310, local copies, waits for them, and re-layouts  32.7 us
    convert_element_type x3, other arithmetic, body(): (first_prev + settings[2 + p] * first_delta).astype(low)  26.7 us
  transfers between devices with their start and end apart: 11, of which 2 were waited for; matrix products, arithmetic and copies ran while one was open for 30% of the time, Pallas kernels for 18%

profile of v1, /device:TPU:1, one launch (start us, length us, event | category | flops | bytes accessed | tf_op | source)
XLA Modules:
  0.0 822.8 jit_solution(10189340555261323219)
XLA Ops:
  8.3 13.4 %all_to_all.40 = bf16[16,5,8,256]{3,0,1,2:T(8,128)(2,1)S(1)} all-to-all(bf16[16,5,8,256]{3,0,1,2:T(8,128)(2,1)S(1)} %bitcast.439), channel_id=1, replica_groups=mesh['z'=4,'x'=4,'y'=4,'core'=2] {'y','core'}, dimensions={2} | all-to-all | bytes 655360 | tf_op jit(solution)/shard_map/all_to_all | solution.py:315
  22.7 23.6 %shard_map.144 = bf16[8,128,2048]{2,1,0:T(8,128)(2,1)} custom-call(bf16[128,2048]{1,0:T(8,128)(2,1)} %bitcast.408), custom_call_target="tpu_custom_call" | custom-call | tf_op jit(solution)/shard_map/pallas_call | solution.py:79
  56.6 17.3 %shard_map.145 = bf16[16,16,128]{2,1,0:T(8,128)(2,1)} custom-call(bf16[16,128]{1,0:T(8,128)(2,1)} %copy-done.112), custom_call_target="tpu_custom_call" | custom-call | tf_op jit(solution)/shard_map/pallas_call | solution.py:222
  84.7 5.8 multiply_add_fusion.4
  98.4 8.7 %add_convert_fusion = (bf16[8,2,64,2048]{3,2,1,0:T(8,128)(2,1)}, f32[8,2,64,2048]{3,2,1,0:T(8,128)S(1)}) fusion(f32[2048]{0:T(1024)S(1)} %bitcast.495, f32[2048]{0:T(1024)S(1)} %bitcast.469, f32[2048]{0:T(1024)S(1)} %bitcast.445, f32[8,2,64]{2,1,0:T(2,128)S(1)} %rsqrt.53, f32[8,2,64]{2,1,0:T(2,128)S(1)} %div.71, bf16[8,2,64,2048]{3,2,1,0:T(8,128)(2,1)} %bitcast.401, ...), kind=kLoop, calls=%fused_computation.36 | loop fusion | flops 20971520 | bytes 25198592 | tf_op jit(solution)/shard_map/convert_element_type | solution.py:348
  107.2 9.3 %fusion.10 = (bf16[1024,2048]{1,0:T(8,128)(2,1)}, bf16[1024,2048]{1,0:T(8,128)(2,1)}, bf16[1024,2048]{1,0:T(8,128)(2,1)}, bf16[1024,2048]{1,0:T(8,128)(2,1)S(1)}) fusion(f32[8,2,64,2048]{3,2,1,0:T(8,128)S(1)} %get-tuple-element.35, f32[2048]{0:T(1024)S(1)} %bitcast.496, f32[2048]{0:T(1024)S(1)} %bitcast.470, f32[2048]{0:T(1024)S(1)} %bitcast.446, ...), kind=kLoop, calls=%fused_computation.26 | loop fusion | flops 37748736 | bytes 29417472 | tf_op jit(solution)/shard_map/convert_element_type | solution.py:348
  122.3 4.8 convolution_convert_fusion.11
  129.0 5.0 convolution_convert_fusion.13
  149.5 13.5 %shard_map.146 = f32[4,256,128]{2,1,0:T(8,128)} custom-call(f32[256,128]{1,0:T(8,128)} %multiply_add_fusion.18.x_ref), custom_call_target="tpu_custom_call" | custom-call | tf_op jit(solution)/shard_map/pallas_call | solution.py:186
  183.0 6.3 multiply_convert_fusion.4
  189.2 23.6 %shard_map.147 = bf16[8,1024,256]{2,1,0:T(8,128)(2,1)} custom-call(bf16[1024,256]{1,0:T(8,128)(2,1)} %get-tuple-element.44.x_ref), custom_call_target="tpu_custom_call" | custom-call | tf_op jit(solution)/shard_map/pallas_call | solution.py:79
  217.1 9.9 %shard_map.148 = bf16[8,128,256]{2,1,0:T(8,128)(2,1)} custom-call(bf16[8,128,256]{2,1,0:T(8,128)(2,1)} %bitcast.456), custom_call_target="tpu_custom_call" | custom-call | tf_op jit(solution)/shard_map/pallas_call | solution.py:163
  234.7 23.4 %shard_map.149 = bf16[8,128,2048]{2,1,0:T(8,128)(2,1)} custom-call(bf16[128,2048]{1,0:T(8,128)(2,1)} %bitcast.427), custom_call_target="tpu_custom_call" | custom-call | tf_op jit(solution)/shard_map/pallas_call | solution.py:79
  261.1 8.8 %add_convert_fusion.1 = (bf16[8,2,64,2048]{3,2,1,0:T(8,128)(2,1)}, bf16[8,2,64,2048]{3,2,1,0:T(8,128)(2,1)}) fusion(f32[8,2,64,2048]{3,2,1,0:T(8,128)} %copy-done.4, f32[2048]{0:T(1024)S(1)} %bitcast.490, f32[2048]{0:T(1024)S(1)} %bitcast.471, f32[2048]{0:T(1024)S(1)} %bitcast.447, f32[8,2,64]{2,1,0:T(2,128)S(1)} %copy-done.72, ...), kind=kLoop, calls=%fused_computation.37 | loop fusion | flops 25165824 | bytes 21012480 | tf_op jit(solution)/shard_map/convert_element_type | solution.py:348
  278.6 6.4 fusion.3
  284.9 5.4 fusion.5
  290.3 4.5 convolution_convert_fusion.10
  294.9 9.7 %shard_map.150 = bf16[8,128,256]{2,1,0:T(8,128)(2,1)} custom-call(bf16[8,128,256]{2,1,0:T(8,128)(2,1)} %bitcast.455), custom_call_target="tpu_custom_call" | custom-call | tf_op jit(solution)/shard_map/pallas_call | solution.py:163
  306.0 7.4 fusion.19
  315.2 7.2 convolution_convert_fusion
  322.4 23.1 %shard_map.151 = f32[128,2048]{1,0:T(8,128)S(1)} custom-call(bf16[8,128,2048]{2,1,0:T(8,128)(2,1)S(1)} %bitcast.392), custom_call_target="tpu_custom_call" | custom-call | tf_op jit(solution)/shard_map/pallas_call | solution.py:137
  349.5 9.8 %shard_map.153 = bf16[8,128,256]{2,1,0:T(8,128)(2,1)} custom-call(bf16[8,128,256]{2,1,0:T(8,128)(2,1)} %bitcast.430), custom_call_target="tpu_custom_call" | custom-call | tf_op jit(solution)/shard_map/pallas_call | solution.py:163
  359.3 23.6 %shard_map.152 = bf16[8,128,2048]{2,1,0:T(8,128)(2,1)} custom-call(bf16[128,2048]{1,0:T(8,128)(2,1)} %get-tuple-element.75.x_ref), custom_call_target="tpu_custom_call" | custom-call | tf_op jit(solution)/shard_map/pallas_call | solution.py:79
  382.9 7.5 convolution_convert_fusion.1
  390.4 6.7 multiply_convert_fusion
  397.1 5.8 convolution_convert_fusion.2
  404.3 9.0 %fusion.17 = f32[1024,2048]{1,0:T(8,128)} fusion(bf16[1024,896]{1,0:T(8,128)(2,1)S(1)} %multiply_convert_fusion, bf16[2048,2048]{1,0:T(8,128)(2,1)} %all-gather.5.cloned.1.call-done), kind=kOutput, calls=%fused_computation.56 | convolution fusion | flops 3758096384 | bytes 13893632 | tf_op jit(solution)/shard_map/dot_general | solution.py:288
  413.3 10.4 %multiply_reduce_fusion = (f32[2048]{0:T(1024)}, f32[2048]{0:T(1024)}, f32[1024,2048]{1,0:T(8,128)S(1)}, f32[1024,2048]{1,0:T(8,128)}) fusion(bf16[8,128,2048]{2,1,0:T(8,128)(2,1)S(1)} %copy-done.2, bf16[8,2,63,2048]{3,2,1,0:T(8,128)(2,1)S(1)} %bitcast.398, bf16[8,2,1,2048]{3,2,1,0:T(2,128)(2,1)S(1)} %copy.271, f32[1024,2048]{1,0:T(8,128)} %fusion.17, ...), kind=kOutput, calls=%fused_computation.30 | convolution fusion | flops 1107292160 | bytes 35176448 | tf_op jit(solution)/shard_map/dot_general | solution.py:288
  425.0 6.1 pad_maximum_fusion.1
  435.8 8.4 %pad_maximum_fusion.2 = f32[8,2,64,2048]{3,2,1,0:T(8,128)} fusion(f32[8,2,1,2048]{3,2,1,0:T(1,128)S(1)} %broadcast_in_dim.48, f32[8,2,63,2048]{3,2,1,0:T(8,128)} %slice.302), kind=kLoop, calls=%fused_computation.2 | loop fusion | flops 2097152 | bytes 16777216 | tf_op jit(solution)/shard_map/concatenate | solution.py:439
  444.1 7.2 fusion.1.p_ref
  451.4 22.9 %shard_map.154 = f32[128,2048]{1,0:T(8,128)S(1)} custom-call(bf16[8,128,2048]{2,1,0:T(8,128)(2,1)S(1)} %fusion.1.p_ref), custom_call_target="tpu_custom_call" | custom-call | tf_op jit(solution)/shard_map/pallas_call | solution.py:137
  476.8 9.8 %shard_map.155 = bf16[8,128,256]{2,1,0:T(8,128)(2,1)} custom-call(bf16[8,128,256]{2,1,0:T(8,128)(2,1)} %bitcast.432), custom_call_target="tpu_custom_call" | custom-call | tf_op jit(solution)/shard_map/pallas_call | solution.py:163
  489.2 23.1 %shard_map.156 = f32[1024,256]{1,0:T(8,128)S(1)} custom-call(bf16[8,1024,256]{2,1,0:T(8,128)(2,1)S(1)} %convert_bitcast_fusion.p_ref), custom_call_target="tpu_custom_call" | custom-call | tf_op jit(solution)/shard_map/pallas_call | solution.py:137
  553.1 11.8 %shard_map.157 = f32[4,256,128]{2,1,0:T(8,128)} custom-call(f32[256,128]{1,0:T(8,128)} %multiply_add_fusion.17.x_ref), custom_call_target="tpu_custom_call" | custom-call | tf_op jit(solution)/shard_map/pallas_call | solution.py:186
  603.8 4.7 fusion.24
  616.9 7.8 copy.323
  624.8 12.0 %copy.325 = bf16[2048,2048]{1,0:T(8,128)(2,1)} copy(bf16[2048,2048]{0,1:T(8,128)(2,1)} %pad_maximum_fusion.1) | data formatting | bytes 16777216
  638.5 5.8 fusion.54
  644.4 5.9 fusion.60
  650.4 6.0 fusion.57
  656.5 22.2 %multiply_reduce_fusion.2 = (f32[2048]{0:T(1024)}, f32[2048]{0:T(1024)}, f32[2048]{0:T(1024)}, f32[2048]{0:T(1024)}, f32[1024,2048]{1,0:T(8,128)}, /*index=5*/f32[1024,2048]{1,0:T(8,128)}) fusion(f32[8,2,64,2048]{3,2,1,0:T(8,128)} %copy-done.4, f32[2048]{0:T(1024)S(1)} %bitcast.472, f32[2048]{0:T(1024)S(1)} %bitcast.448, f32[1024]{0:T(1024)S(1)} %copy-done.111, ...), kind=kOutput, calls=%fused_computation.32 | convolution fusion | flops 1132453888 | bytes 56221696 | tf_op jit(solution)/shard_map/dot_general | solution.py:288
  688.7 4.5 slice.313
  697.7 9.4 %fusion.p_ref = bf16[8,128,2048]{2,1,0:T(8,128)(2,1)} fusion(f32[8,128,2048]{2,1,0:T(8,128)} %bitcast.412, f32[8,2,64,2048]{3,2,1,0:T(8,128)} %pad_maximum_fusion.3), kind=kLoop, calls=%fused_computation.6 | loop fusion | flops 4194304 | bytes 20971520 | tf_op jit(solution)/shard_map/convert_element_type | solution.py:530
  709.4 23.6 %shard_map.158 = f32[128,2048]{1,0:T(8,128)S(1)} custom-call(bf16[8,128,2048]{2,1,0:T(8,128)(2,1)S(1)} %copy-done), custom_call_target="tpu_custom_call" | custom-call | tf_op jit(solution)/shard_map/pallas_call | solution.py:137
  751.2 36.9 %reduce-scatter.9.cloned.1.call-done = bf16[128,2048]{1,0:T(8,128)(2,1)} async-done(((bf16[2048,2048]{1,0:T(8,128)(2,1)}), bf16[128,2048]{1,0:T(8,128)(2,1)}) %reduce-scatter.9.cloned.1.call-update) | async-done | bytes 524304 | tf_op jit(solution)/shard_map/reduce_scatter | solution.py:450
  788.0 6.2 all-to-all-start.3
  795.8 15.4 %shard_map.159 = f32[16,128]{1,0:T(8,128)} custom-call(f32[16,16,128]{2,1,0:T(8,128)} %bitcast_bitcast_fusion.x_ref), custom_call_target="tpu_custom_call" | custom-call | tf_op jit(solution)/shard_map/pallas_call | solution.py:252
  (544 shorter events, 246.8 us)
Async XLA Ops:
  7.2 43.1 %copy-start.85 = (bf16[16,2048]{1,0:T(8,128)(2,1)S(1)}, bf16[16,2048]{1,0:T(8,128)(2,1)}, u32[]{:S(2)}) copy-start(bf16[16,2048]{1,0:T(8,128)(2,1)} %param.13) | copy-start | bytes 196612
  7.2 43.1 %copy-start.64 = (bf16[16,7168]{1,0:T(8,128)(2,1)S(1)}, bf16[16,7168]{1,0:T(8,128)(2,1)}, u32[]{:S(2)}) copy-start(bf16[16,7168]{1,0:T(8,128)(2,1)} %param.12) | copy-start | bytes 688132
  7.2 84.4 %all-gather.3.cloned.1.call-start = ((), (), s32[]{:S(2)}) async-start(), calls=%async_computation.6 | async-start | bytes 5570560 | tf_op jit(solution)/shard_map/all_gather | solution.py:316
  8.3 42.0 %copy-start.65 = (bf16[16,7168]{1,0:T(8,128)(2,1)S(1)}, bf16[16,7168]{1,0:T(8,128)(2,1)}, u32[]{:S(2)}) copy-start(bf16[16,7168]{1,0:T(8,128)(2,1)} %param.11) | copy-start | bytes 688132
  22.7 32.7 %copy-start.134 = (bf16[13,16]{1,0:T(8,128)(2,1)S(1)}, bf16[13,16]{1,0:T(8,128)(2,1)}, u32[]{:S(2)}) copy-start(bf16[13,16]{1,0:T(8,128)(2,1)} %param.14) | copy-start | bytes 1252
  47.1 50.6 %collective-permute-start = (bf16[2,2048]{1,0:T(2,128)(2,1)S(1)}, bf16[2,2048]{1,0:T(2,128)(2,1)S(1)}, u32[]{:S(2)}, u32[]{:S(2)}) collective-permute-start(bf16[2,2048]{1,0:T(2,128)(2,1)S(1)} %bitcast.515), channel_id=1, source_target_pairs={{0,8},{8,16},{16,24},{1,9},{9,17},{17,25},{2,10},{10,18},{18,26},{... | collective-permute-start | bytes 24584 | tf_op jit(solution)/shard_map/ppermute | solution.py:264
  51.5 40.1 %all-to-all-start = ((bf16[16,8,2048]{2,0,1:T(8,128)(2,1)}), bf16[16,8,2048]{2,0,1:T(8,128)(2,1)S(1)}, u32[]{:S(2)}, u32[]{:S(2)}) async-start(bf16[16,8,2048]{2,0,1:T(8,128)(2,1)} %copy.247), calls=%async_computation | async-start | bytes 1048576 | tf_op jit(solution)/shard_map/all_to_all | solution.py:325
  55.4 235.0 %all-gather.5.cloned.1.call-start = ((), (), s32[]{:S(2)}) async-start(), calls=%async_computation.7 | async-start | bytes 8912896 | tf_op jit(solution)/shard_map/all_gather | solution.py:328
  76.9 30.2 %copy-start.108 = (f32[1024]{0:T(1024)}, f32[1024]{0:T(1024)S(1)}, u32[]{:S(2)}) copy-start(f32[1024]{0:T(1024)S(1)} %get-tuple-element.115) | copy-start | bytes 12292
  80.4 26.7 %copy-start.110 = (f32[1024]{0:T(1024)}, f32[1024]{0:T(1024)S(1)}, u32[]{:S(2)}) copy-start(f32[1024]{0:T(1024)S(1)} %get-tuple-element.117) | copy-start | bytes 12292
  84.7 176.4 %copy-start.56 = (f32[1,16,128]{2,0,1:T(1,128)}, f32[1,16,128]{2,0,1:T(1,128)S(1)}, u32[]{:S(2)}) copy-start(f32[1,16,128]{2,0,1:T(1,128)S(1)} %get-tuple-element.112) | copy-start | bytes 24580
  84.7 176.4 %copy-start.61 = (f32[1,16,128]{2,0,1:T(1,128)}, f32[1,16,128]{2,0,1:T(1,128)S(1)}, u32[]{:S(2)}) copy-start(f32[1,16,128]{2,0,1:T(1,128)S(1)} %get-tuple-element.111) | copy-start | bytes 24580
  92.4 644.4 %reduce-scatter.7.cloned.1.call-start = ((), (), s32[]{:S(2)}) async-start(), calls=%async_computation.8 | async-start | bytes 5570560 | tf_op jit(solution)/shard_map/reduce_scatter | solution.py:518
  96.9 51.9 %copy-start.50 = (f32[256,128]{1,0:T(8,128)}, f32[256,128]{1,0:T(8,128)S(1)}, u32[]{:S(2)}) copy-start(f32[256,128]{1,0:T(8,128)S(1)} %mul.1380) | copy-start | bytes 393220
  97.1 51.7 %copy-start.52 = (f32[256,128]{1,0:T(8,128)}, f32[256,128]{1,0:T(8,128)S(1)}, u32[]{:S(2)}) copy-start(f32[256,128]{1,0:T(8,128)S(1)} %mul.1373) | copy-start | bytes 393220
  122.3 51.0 %copy-start.8 = (bf16[8,2,64,4,64]{2,4,3,1,0:T(8,128)(2,1)}, bf16[8,2,64,4,64]{2,4,3,1,0:T(8,128)(2,1)S(1)}, u32[]{:S(2)}) copy-start(bf16[8,2,64,4,64]{2,4,3,1,0:T(8,128)(2,1)S(1)} %copy.252) | copy-start | bytes 1572868
  129.0 42.1 %copy-start.6 = (bf16[8,2,64,4,64]{2,4,3,1,0:T(8,128)(2,1)}, bf16[8,2,64,4,64]{2,4,3,1,0:T(8,128)(2,1)S(1)}, u32[]{:S(2)}) copy-start(bf16[8,2,64,4,64]{2,4,3,1,0:T(8,128)(2,1)S(1)} %copy.254) | copy-start | bytes 1572868
  174.0 97.1 %copy-start.5 = (f32[8,2,64,4,64]{2,4,3,1,0:T(8,128)}, f32[8,2,64,4,64]{2,4,3,1,0:T(8,128)S(1)}, u32[]{:S(2)}) copy-start(f32[8,2,64,4,64]{2,4,3,1,0:T(8,128)S(1)} %get-tuple-element.132) | copy-start | bytes 3145732
  233.4 27.7 %copy-start.70 = (f32[8,2,64]{2,1,0:T(2,128)S(1)}, f32[8,2,64]{2,1,0:T(2,128)}, u32[]{:S(2)}) copy-start(f32[8,2,64]{2,1,0:T(2,128)} %copy-done.69) | copy-start | bytes 12292
  233.4 27.7 %copy-start.72 = (f32[8,2,64]{2,1,0:T(2,128)S(1)}, f32[8,2,64]{2,1,0:T(2,128)}, u32[]{:S(2)}) copy-start(f32[8,2,64]{2,1,0:T(2,128)} %copy-done.71) | copy-start | bytes 12292
  233.4 27.7 %copy-start.78 = (f32[1,16,128]{2,0,1:T(1,128)S(1)}, f32[1,16,128]{2,0,1:T(1,128)}, u32[]{:S(2)}) copy-start(f32[1,16,128]{2,0,1:T(1,128)} %copy-done.77) | copy-start | bytes 24580
  233.4 27.7 %copy-start.81 = (f32[1,16,128]{2,0,1:T(1,128)S(1)}, f32[1,16,128]{2,0,1:T(1,128)}, u32[]{:S(2)}) copy-start(f32[1,16,128]{2,0,1:T(1,128)} %copy-done.80) | copy-start | bytes 24580
  233.4 24.8 %copy-start.86 = (f32[2,64]{1,0:T(2,128)}, f32[2,64]{1,0:T(2,128)S(1)}, u32[]{:S(2)}) copy-start(f32[2,64]{1,0:T(2,128)S(1)} %broadcast_multiply_fusion.8) | copy-start | bytes 1540
  233.6 24.5 %copy-start.103 = (f32[2,64]{1,0:T(2,128)}, f32[2,64]{1,0:T(2,128)S(1)}, u32[]{:S(2)}) copy-start(f32[2,64]{1,0:T(2,128)S(1)} %add_rsqrt_fusion.3) | copy-start | bytes 1540
  259.1 19.3 %collective-permute-start.1 = (bf16[2,2048]{1,0:T(2,128)(2,1)S(1)}, bf16[2,2048]{1,0:T(2,128)(2,1)S(1)}, u32[]{:S(2)}, u32[]{:S(2)}) collective-permute-start(bf16[2,2048]{1,0:T(2,128)(2,1)S(1)} %bitcast.516), channel_id=1, source_target_pairs={{0,8},{8,16},{16,24},{1,9},{9,17},{17,25},{2,10},{10,18},{18,26},{... | collective-permute-start | bytes 24584 | tf_op jit(solution)/shard_map/ppermute | solution.py:264
  423.7 11.9 %collective-permute-start.2 = (f32[2,2048]{1,0:T(2,128)S(1)}, f32[2,2048]{1,0:T(2,128)S(1)}, u32[]{:S(2)}, u32[]{:S(2)}) collective-permute-start(f32[2,2048]{1,0:T(2,128)S(1)} %bitcast.514), channel_id=1, source_target_pairs={{8,0},{16,8},{24,16},{9,1},{17,9},{25,17},{10,2},{18,10},{26,18},{... | collective-permute-start | bytes 49160 | tf_op jit(solution)/shard_map/ppermute | solution.py:264
  451.4 23.9 %copy-start.25 = (bf16[2,64,2048]{2,1,0:T(8,128)(2,1)S(1)}, bf16[2,64,2048]{2,1,0:T(8,128)(2,1)}, u32[]{:S(2)}) copy-start(bf16[2,64,2048]{2,1,0:T(8,128)(2,1)} %param.17) | copy-start | bytes 1572868
  451.4 23.9 %copy-start.116 = (f32[2,64]{1,0:T(2,128)S(1)}, f32[2,64]{1,0:T(2,128)}, u32[]{:S(2)}) copy-start(f32[2,64]{1,0:T(2,128)} %copy-done.115) | copy-start | bytes 1540
  486.6 25.6 %copy-start.54 = (f32[1024,256]{1,0:T(8,128)S(1)}, f32[1024,256]{1,0:T(8,128)}, u32[]{:S(2)}) copy-start(f32[1024,256]{1,0:T(8,128)} %get-tuple-element.45) | copy-start | bytes 3145732
  486.6 25.6 %copy-start.55 = (f32[1024,256]{1,0:T(8,128)S(1)}, f32[1024,256]{1,0:T(8,128)}, u32[]{:S(2)}) copy-start(f32[1024,256]{1,0:T(8,128)} %get-tuple-element.133) | copy-start | bytes 3145732
  486.6 25.6 %copy-start.136 = (f32[1,256]{1,0:T(1,128)S(1)}, f32[1,256]{1,0:T(1,128)}, u32[]{:S(2)}) copy-start(f32[1,256]{1,0:T(1,128)} %get-tuple-element.41) | copy-start | bytes 3076
  486.6 25.6 %copy-start.138 = (f32[1,256]{1,0:T(1,128)S(1)}, f32[1,256]{1,0:T(1,128)}, u32[]{:S(2)}) copy-start(f32[1,256]{1,0:T(1,128)} %get-tuple-element.114) | copy-start | bytes 3076
  538.1 32.1 %copy-start.75 = (f32[4]{0:T(128)S(1)}, f32[4]{0:T(128)}, u32[]{:S(2)}) copy-start(f32[4]{0:T(128)} %copy-done.73) | copy-start | bytes 52
  624.7 163.3 %reduce-scatter.9.cloned.1.call-start = ((), (), s32[]{:S(2)}) async-start(), calls=%async_computation.9 | async-start | bytes 8912896 | tf_op jit(solution)/shard_map/reduce_scatter | solution.py:450
  637.5 96.4 %copy-start.118 = (f32[2,64]{1,0:T(2,128)}, f32[2,64]{1,0:T(2,128)S(1)}, u32[]{:S(2)}) copy-start(f32[2,64]{1,0:T(2,128)S(1)} %add_rsqrt_fusion.2) | copy-start | bytes 1540
  656.5 24.5 %copy-start.45 = (f32[8,2,64,4]{3,2,1,0:T(8,128)S(1)}, f32[8,2,64,4]{3,2,1,0:T(8,128)}, u32[]{:S(2)}) copy-start(f32[8,2,64,4]{3,2,1,0:T(8,128)} %copy.335) | copy-start | bytes 49156
  679.7 13.6 %collective-permute-start.3 = (f32[2,2048]{1,0:T(2,128)S(1)}, f32[2,2048]{1,0:T(2,128)S(1)}, u32[]{:S(2)}, u32[]{:S(2)}) collective-permute-start(f32[2,2048]{1,0:T(2,128)S(1)} %bitcast.513), channel_id=1, source_target_pairs={{8,0},{16,8},{24,16},{9,1},{17,9},{25,17},{10,2},{18,10},{26,18},{... | collective-permute-start | bytes 49160 | tf_op jit(solution)/shard_map/ppermute | solution.py:264
  709.3 24.5 %copy-start.114 = (f32[2,64]{1,0:T(2,128)S(1)}, f32[2,64]{1,0:T(2,128)}, u32[]{:S(2)}) copy-start(f32[2,64]{1,0:T(2,128)} %broadcast_multiply_fusion.5) | copy-start | bytes 1540
  709.3 26.0 %copy-start.97 = (f32[2048]{0:T(1024)S(1)}, f32[2048]{0:T(1024)}, u32[]{:S(2)}) copy-start(f32[2048]{0:T(1024)} %get-tuple-element.19) | copy-start | bytes 24580
  709.3 26.0 %copy-start.98 = (f32[2048]{0:T(1024)S(1)}, f32[2048]{0:T(1024)}, u32[]{:S(2)}) copy-start(f32[2048]{0:T(1024)} %get-tuple-element.20) | copy-start | bytes 24580
  709.3 26.0 %copy-start.99 = (f32[2048]{0:T(1024)S(1)}, f32[2048]{0:T(1024)}, u32[]{:S(2)}) copy-start(f32[2048]{0:T(1024)} %get-tuple-element.21) | copy-start | bytes 24580
  709.3 26.0 %copy-start.100 = (f32[2048]{0:T(1024)S(1)}, f32[2048]{0:T(1024)}, u32[]{:S(2)}) copy-start(f32[2048]{0:T(1024)} %get-tuple-element.26) | copy-start | bytes 24580
  709.3 26.0 %copy-start.125 = (f32[2048]{0:T(1024)S(1)}, f32[2048]{0:T(1024)}, u32[]{:S(2)}) copy-start(f32[2048]{0:T(1024)} %get-tuple-element.15) | copy-start | bytes 24580
  709.3 26.0 %copy-start.126 = (f32[2048]{0:T(1024)S(1)}, f32[2048]{0:T(1024)}, u32[]{:S(2)}) copy-start(f32[2048]{0:T(1024)} %get-tuple-element.16) | copy-start | bytes 24580
  709.3 26.0 %copy-start.127 = (f32[2048]{0:T(1024)S(1)}, f32[2048]{0:T(1024)}, u32[]{:S(2)}) copy-start(f32[2048]{0:T(1024)} %get-tuple-element.17) | copy-start | bytes 24580
  709.4 26.0 %copy-start.128 = (f32[2048]{0:T(1024)S(1)}, f32[2048]{0:T(1024)}, u32[]{:S(2)}) copy-start(f32[2048]{0:T(1024)} %get-tuple-element.18) | copy-start | bytes 24580
  740.8 10.4 %all-to-all-start.2 = ((bf16[8,16,5,256]{3,1,2,0:T(8,128)(2,1)}), bf16[8,16,5,256]{3,1,2,0:T(8,128)(2,1)S(1)}, u32[]{:S(2)}, u32[]{:S(2)}) async-start(bf16[8,16,5,256]{3,1,2,0:T(8,128)(2,1)} %copy.303), calls=%async_computation.2 | async-start | bytes 655360 | tf_op jit(solution)/shard_map/all_to_all | solution.py:519
  788.0 25.5 %all-to-all-start.3 = ((bf16[8,16,2048]{2,1,0:T(8,128)(2,1)}), bf16[8,16,2048]{2,1,0:T(8,128)(2,1)S(1)}, u32[]{:S(2)}, u32[]{:S(2)}) async-start(bf16[8,16,2048]{2,1,0:T(8,128)(2,1)} %bitcast.454), calls=%async_computation.3 | async-start | bytes 1048576 | tf_op jit(solution)/shard_map/all_to_all | solution.py:451
  (108 other events, 845.7 us)
Sparse Core Ops, SparseCore 0:
  22.8 57.5 all-gather.2
  92.6 73.8 all-gather.4
  624.9 75.6 reduce-scatter.6
  703.9 84.1 reduce-scatter.8

commit v2 on v0

v2 whole, which is shorter than its diff:
```python
import jax
import jax.numpy as jnp
from jax import lax
from jax.experimental import pallas as pl
from jax.experimental.pallas import tpu as pltpu
from jax.sharding import Mesh, PartitionSpec as P

BLOCK_LEN = 64
epsilon = 1e-05
group_epsilon = 0.00064

GROUP = ("y", "core")
ROWS = ("z", "x")
SEQ = ("x", "y", "core")
ALL = ("z", "x", "y", "core")
low = jnp.bfloat16


MESH = pl.DeviceIdType.MESH
HBM = pl.BlockSpec(memory_space=pl.ANY)


def cost(microseconds):
    return pl.CostEstimate(flops=0, bytes_accessed=microseconds * 3_000_000, transcendentals=0)


VMEM = pl.BlockSpec(memory_space=pltpu.VMEM)


def greet(devices):
    barrier = pltpu.get_barrier_semaphore()
    for device in devices:
        pl.semaphore_signal(barrier, inc=1, device_id=device, device_id_type=MESH)
    pl.semaphore_wait(barrier, len(devices))

def ring_places():
    y, c = lax.axis_index("y"), lax.axis_index("core")
    right, left, far = lax.rem(y + 1, 4), lax.rem(y + 3, 4), lax.rem(y + 2, 4)
    return y, c, right, left, far

def cube_places():
    z, x, y, c = [lax.axis_index(name) for name in ("z", "x", "y", "core")]
    place, member = z * 4 + x, y * 2 + c
    far = [lax.rem(place + k, 16) for k in range(1, 16)]
    near = [lax.rem(member + k, 8) for k in range(1, 8)]
    return place, member, far, near, [{"z": p // 4, "x": lax.rem(p, 4)} for p in far], [{"y": p // 2, "core": lax.rem(p, 2)} for p in near]

def nn(left, right):
    return jnp.dot(left, right, preferred_element_type=jnp.float32)


def nt(left, right):
    return lax.dot_general(left, right, (((1,), (1,)), ((), ())), preferred_element_type=jnp.float32)


def tn(left, right):
    return lax.dot_general(left, right, (((0,), (0,)), ((), ())), preferred_element_type=jnp.float32)


def head_tables(log_row):
    width = log_row.shape[-1]
    place = lax.broadcasted_iota(jnp.int32, (BLOCK_LEN, width), 0)
    other = lax.rem(lax.broadcasted_iota(jnp.int32, (BLOCK_LEN, width), 1), BLOCK_LEN)
    gap = jnp.maximum(place - 1 - other, 0).astype(jnp.float32)
    mask = jnp.where(other < place, jnp.exp(gap * log_row), 0.0)
    eye = other == place
    enter = jnp.exp(place.astype(jnp.float32) * log_row)
    leave = jnp.exp((BLOCK_LEN - 1 - place).astype(jnp.float32) * log_row)
    tall = lax.broadcasted_iota(jnp.int32, (width, width), 0) // BLOCK_LEN
    wide = lax.broadcasted_iota(jnp.int32, (width, width), 1) // BLOCK_LEN
    return mask, eye, enter, leave, tall == wide


def expand(block, same):
    copies = block.shape[1] // BLOCK_LEN
    return jnp.where(same, jnp.concatenate([block] * copies, axis=0), jnp.zeros((), block.dtype))


def compress(square, same):
    kept = jnp.where(same, square, 0.0)
    return sum(kept[k * BLOCK_LEN : (k + 1) * BLOCK_LEN] for k in range(square.shape[0] // BLOCK_LEN))


def head_sum(values, same, factor=1.0):
    ones = jnp.where(same, factor, 0.0).astype(low)
    high = values.astype(low)
    rest = (values - high.astype(jnp.float32)).astype(low)
    return nn(high, ones) + nn(rest, ones)


def head_mean(values, same):
    return head_sum(values, same, 1.0 / BLOCK_LEN)


def block_rows(m, s):
    return pl.ds(pl.multiple_of(m * 2 * BLOCK_LEN + s * BLOCK_LEN, BLOCK_LEN), BLOCK_LEN)


def start_line(total, slots, send, recv):
    me = lax.axis_index("x")
    devices = [{"x": lax.rem(me + k, 4)} for k in range(1, 4)]
    slots[me] = total[...]
    copies = [
        pltpu.make_async_remote_copy(
            src_ref=total, dst_ref=slots.at[me], send_sem=send.at[k], recv_sem=recv.at[k], device_id=d, device_id_type=MESH
        )
        for k, d in enumerate(devices)
    ]
    for one in copies:
        one.start()
    return copies


def recurrence_kernel(
    r_ref, k_ref, v_ref, g_ref, p_ref, tok_ref, set_ref, time_hbm,
    w_ref, scaled_ref, inverse_ref, in_ref, hidden_ref, second_ref, gated_ref,
    wkv, prefix, total, slots, gated, time, out, out_all, send, recv, local,
):
    x, member, near, near_devices, _, _ = group_and_line()
    y, c, right, left, far = ring_places()
    greet(near_devices + [{"x": lax.rem(x + n, 4)} for n in range(1, 4)])
    copy = Copies(send, recv)
    load = pltpu.make_async_copy(time_hbm.at[4], time, local.at[0])
    load.start()
    log_row, bonus, gain, bias = [p_ref[n : n + 1, :] for n in range(4)]
    mask, eye, enter, leave, same = head_tables(log_row)
    block_decay = jnp.exp(BLOCK_LEN * log_row)

    def first(m, states):
        after = []
        for s in range(2):
            rows = block_rows(m, s)
            r, k, v = r_ref[rows], k_ref[rows], v_ref[rows]
            key = expand(k, same)
            scores = nt(r, key)
            pairs = head_sum(r.astype(jnp.float32) * bonus * k.astype(jnp.float32), same)
            weights = (scores * mask + jnp.where(eye, pairs, 0.0)).astype(low)
            w_ref[rows] = weights
            wkv[rows] = nn(weights, expand(v, same))
            prefix[m * 2 + s] = states[s]
            key_leave = (k.astype(jnp.float32) * leave).astype(low)
            after.append(states[s] * block_decay + compress(tn(key_leave, v), same))
        return tuple(after)

    zero = jnp.zeros(enter.shape, jnp.float32)
    states = lax.fori_loop(0, 8, first, (zero, zero))
    for s in range(2):
        total[s] = states[s]
    for one in start_line(total, slots, send.at[pl.ds(30, 3)], recv.at[pl.ds(30, 3)]):
        one.wait()
    x_place = lax.axis_index("x")
    entering = [zero, zero]
    span_decay = jnp.exp(8.0 * BLOCK_LEN * log_row)
    for x in range(3):
        for s in range(2):
            entering[s] = jnp.where(x < x_place, entering[s] * span_decay + slots[x, s], entering[s])
    for s in range(2):
        total[s] = entering[s]

    def second(m, carry):
        power = jnp.exp((m * BLOCK_LEN).astype(jnp.float32) * log_row)
        for s in range(2):
            rows = block_rows(m, s)
            state = (prefix[m * 2 + s] + power * total[s]).astype(low)
            in_ref[m * 2 + s] = state
            recv_enter = (r_ref[rows].astype(jnp.float32) * enter).astype(low)
            out = wkv[rows] + nn(recv_enter, expand(state, same))
            center = out - head_mean(out, same)
            inverse = lax.rsqrt(head_mean(center * center, same) + group_epsilon)
            scaled = center * inverse
            scaled_ref[rows] = scaled
            inverse_ref[rows] = inverse
            gate = g_ref[rows]
            gated[member, rows] = ((scaled * gain + bias) * gate * jax.nn.sigmoid(gate)).astype(low)
        return carry

    half = gated.shape[1] // 2
    ring = Ring(copy, "y", lambda at, n: gated.at[at * 2 + c, pl.ds(n * half, half)], start=False)
    to_sibling = {"core": 1 - c}
    across = [copy(gated.at[member, pl.ds(n * half, half)], gated.at[member, pl.ds(n * half, half)], to_sibling) for n in range(2)]
    for n in range(2):
        lax.fori_loop(4 * n, 4 * n + 4, second, 0)
        ring.start(n)
        across[n].start()

    def pass_on(at):
        one = copy(gated.at[at * 2 + c], gated.at[at * 2 + c], to_sibling)
        one.start()
        return one

    ring.forward()
    ring.wait_near()
    passed = [pass_on(right), pass_on(left)]
    load.wait()
    ring.wait_far()
    passed.append(pass_on(far))
    for one in across + passed:
        one.wait_recv()
    keep = pltpu.make_async_copy(gated, gated_ref, local.at[1])
    keep.start()

    cols = w_ref.shape[1]
    given = []

    def project(q):
        rows = pl.ds(pl.multiple_of(q * 256, 256), 256)
        value = sum(nn(gated[m, rows], time[m * cols : (m + 1) * cols]) for m in range(8)).astype(low)
        for b in range(2):
            out[q * 2 + b] = value[b * 128 : (b + 1) * 128]

    for at in (far, right, left, y):
        project(at)
        for turn in range(2):
            j = at * 2 + lax.rem(c + turn, 2)
            if at is y and turn == 0:
                continue
            given.append(copy(out.at[j], out_all.at[member], {"y": at, "core": lax.rem(c + turn, 2)}))
            given[-1].start()
    out_all[member] = out[member]
    for one in given:
        one.wait_recv()

    def norm_rows(t, carry):
        rows = pl.ds(pl.multiple_of(t * 16, 16), 16)
        added = jnp.concatenate([out_all[n, rows].astype(jnp.float32) for n in range(8)], axis=1)
        values = tok_ref[rows].astype(jnp.float32) + added
        hidden_ref[rows] = values
        center = values - jnp.mean(values, axis=-1, keepdims=True)
        inverse = lax.rsqrt(jnp.mean(center * center, axis=-1, keepdims=True) + epsilon)
        second_ref[rows] = (center * inverse * set_ref[9:10, :] + set_ref[10:11, :]).astype(low)
        return carry

    lax.fori_loop(0, 8, norm_rows, 0)
    copy.wait_sent()
    keep.wait()


def recurrence(r, k, v, g, params, tokens, settings, time, cid):
    rows, cols = r.shape
    own_rows, width = tokens.shape
    shape = jax.ShapeDtypeStruct
    return pl.pallas_call(
        recurrence_kernel,
        name="recurrence",
        cost_estimate=cost(55),
        out_shape=[
            shape((rows, cols), low),
            shape((rows, cols), jnp.float32),
            shape((rows, cols), jnp.float32),
            shape((16, BLOCK_LEN, cols), low),
            shape((own_rows, width), jnp.float32),
            shape((own_rows, width), low),
            shape((8, rows, cols), low),
        ],
        in_specs=[VMEM] * 7 + [HBM],
        out_specs=[VMEM] * 6 + [HBM],
        scratch_shapes=[
            pltpu.VMEM((rows, cols), jnp.float32),
            pltpu.VMEM((16, BLOCK_LEN, cols), jnp.float32),
            pltpu.VMEM((2, BLOCK_LEN, cols), jnp.float32),
            pltpu.VMEM((4, 2, BLOCK_LEN, cols), jnp.float32),
            pltpu.VMEM((8, rows, cols), low),
            pltpu.VMEM((width, cols), low),
            pltpu.VMEM((8, own_rows, cols), low),
            pltpu.VMEM((8, own_rows, cols), low),
            pltpu.SemaphoreType.DMA((33,)),
            pltpu.SemaphoreType.DMA((33,)),
            pltpu.SemaphoreType.DMA((2,)),
        ],
        compiler_params=pltpu.CompilerParams(collective_id=cid, has_side_effects=True, vmem_limit_bytes=48 * 2**20),
    )(r, k, v, g, params, tokens, settings, time)


class Copies:
    def __init__(self, send, recv):
        self.send, self.recv, self.count, self.all = send, recv, 0, []

    def __call__(self, src, dst, device):
        one = pltpu.make_async_remote_copy(
            src_ref=src,
            dst_ref=dst,
            send_sem=self.send.at[self.count],
            recv_sem=self.recv.at[self.count],
            device_id=device,
            device_id_type=MESH,
        )
        self.count += 1
        self.all.append(one)
        return one

    def wait_sent(self, some=None):
        some = self.all if some is None else some
        for one in some:
            one.wait_send()
        self.all = [one for one in self.all if not any(one is other for other in some)]


class Ring:
    def __init__(self, copy, axis, part, start=True):
        me = lax.axis_index(axis)
        self.copy, self.part = copy, part
        self.right, self.left, self.far = [lax.rem(me + k, 4) for k in (1, 3, 2)]
        self.to_right, self.to_left = {axis: self.right}, {axis: self.left}
        own = [part(me, 0), part(me, 1)]
        self.near = [
            copy(own[0], own[0], self.to_right),
            copy(own[1], own[1], self.to_left),
            copy(own[1], own[1], self.to_right),
            copy(own[0], own[0], self.to_left),
        ]
        if start:
            for one in self.near:
                one.start()

    def start(self, half):
        for n in ((0, 3), (2, 1))[half]:
            self.near[n].start()

    def forward(self):
        self.near[0].wait_recv()
        there = self.part(self.left, 0)
        self.far_right = self.copy(there, there, self.to_right)
        self.far_right.start()
        self.near[1].wait_recv()
        there = self.part(self.right, 1)
        self.far_left = self.copy(there, there, self.to_left)
        self.far_left.start()

    def wait_near(self):
        self.near[2].wait_recv()
        self.near[3].wait_recv()

    def wait_far(self):
        self.far_right.wait_recv()
        self.far_left.wait_recv()


def opening_kernel(
    tok_ref, tw_ref, ck_ref, cv_ref, cg_ref, vec_ref,
    r_ref, k_ref, v_ref, g_ref, set_ref, time_ref, prev_ref, delta_ref, stripe_ref,
    tokens, time, mix, prev, delta, vec_blocks, vec_stripe, vec_all, send, recv, local,
):
    place, member, far, near, far_devices, near_devices = cube_places()
    z, x, y, c = [lax.axis_index(name) for name in ("z", "x", "y", "core")]
    greet(far_devices + near_devices)
    copy = Copies(send, recv)
    own = tw_ref.shape[2] // 8
    wide = ck_ref.shape[1] // 8

    def lanes(p, size):
        return pl.ds(pl.multiple_of(p * size, size), size)

    def tile(p):
        return pl.ds(pl.multiple_of(p * 16, 16), 16)

    vec_near = [copy(vec_ref, vec_blocks.at[n], d) for n, d in enumerate(near_devices)]
    for one in vec_near:
        one.start()
    time_near = [
        copy(tw_ref.at[:, :, lanes(p, own)], time.at[:, z, x, tile(member), :], d) for p, d in zip(near, near_devices)
    ]
    for one in time_near:
        one.start()
    time_own = pltpu.make_async_copy(tw_ref.at[:, :, lanes(member, own)], time.at[:, z, x, tile(member), :], local.at[0])
    time_own.start()
    tokens[member] = tok_ref[...]
    gathered = Tokens(copy, tokens, member)
    to_next = {"x": lax.rem(x + 1, 4)}
    last_rows = [pl.ds(s * BLOCK_LEN + BLOCK_LEN - 16, 16) for s in range(2)]
    edges = [copy(tokens.at[7, rows], tokens.at[8, rows], to_next) for rows in last_rows]

    total = vec_ref[...].astype(jnp.float32)
    for n, one in enumerate(vec_near):
        one.wait_recv()
        total = total + vec_blocks[n].astype(jnp.float32)
    vec_stripe[...] = total.astype(low)
    vec_all[place] = vec_stripe[...]
    vec_far = [copy(vec_stripe, vec_all.at[place], d) for d in far_devices]
    for one in vec_far:
        one.start()

    for one in time_near:
        one.wait_recv()
    time_own.wait()
    one_side, other_side = pl.ds(0, own // 2), pl.ds(own // 2, own // 2)
    rows = time.shape[3] // 2
    z_first = Ring(copy, "z", lambda at, n: time.at[:, at, x, pl.ds(n * rows, rows), one_side])
    x_first = Ring(copy, "x", lambda at, n: time.at[:, z, at, pl.ds(n * rows, rows), other_side])
    gathered.ring.forward()
    z_first.forward()
    x_first.forward()
    z_first.wait_near()
    z_first.wait_far()
    x_last = Ring(copy, "x", lambda at, n: time.at[:, pl.ds(n * 2, 2), at, :, one_side])
    x_first.wait_near()
    x_first.wait_far()
    z_last = Ring(copy, "z", lambda at, n: time.at[:, at, pl.ds(n * 2, 2), :, other_side])
    for one in vec_far:
        one.wait_recv()
    for n in range(16):
        set_ref[:, n * 128 : (n + 1) * 128] = vec_all[n].astype(jnp.float32)
    gathered.wait_next()

    channel = []
    for source, size, start in ((ck_ref, wide, 0), (cv_ref, wide, wide), (cg_ref, own, 2 * wide)):
        for p, d in zip(near, near_devices):
            channel.append(copy(source.at[:, lanes(p, size)], stripe_ref.at[tile(member), pl.ds(start, size)], d))
    for one in channel:
        one.start()
    kept = [
        pltpu.make_async_copy(source.at[:, lanes(member, size)], stripe_ref.at[tile(member), pl.ds(start, size)], local.at[n])
        for n, (source, size, start) in enumerate(((ck_ref, wide, 0), (cv_ref, wide, wide), (cg_ref, own, 2 * wide)))
    ]
    for one in kept:
        one.start()

    width = tok_ref.shape[1]
    step = 512
    row = lax.broadcasted_iota(jnp.int32, (16, step), 0)

    def statistics(values):
        mean = jnp.mean(values, axis=-1, keepdims=True)
        center = values - mean
        return mean, lax.rsqrt(jnp.mean(center * center, axis=-1, keepdims=True) + epsilon)

    def mix_pair(q):
        @pl.when(q == 0)
        def _():
            for one in edges:
                one.wait_recv()

        def mix_block(b, carry):
            j = q * 2 + b
            before_slot = jnp.where(j == 0, 8, j - 1)
            hidden = jnp.logical_and(j == 0, x == 0)
            for s in range(2):
                last = slice(s * BLOCK_LEN + BLOCK_LEN - 16, (s + 1) * BLOCK_LEN)
                found = [statistics(tokens[before_slot, last].astype(jnp.float32))]
                found[0] = (found[0][0][15:16], found[0][1][15:16])
                for t in range(BLOCK_LEN // 16):
                    at = s * BLOCK_LEN + t * 16
                    found.append(statistics(tokens[j, at : at + 16].astype(jnp.float32)))

                def columns(n, carry):
                    cols = pl.ds(pl.multiple_of(n * step, step), step)
                    gain, offset = set_ref[0:1, cols], set_ref[1:2, cols]
                    before = tokens[before_slot, last, cols].astype(jnp.float32)[15:16]
                    before = (before - found[0][0]) * found[0][1] * gain + offset
                    before = jnp.where(hidden, 0.0, before)
                    for t in range(BLOCK_LEN // 16):
                        at = s * BLOCK_LEN + t * 16
                        mean, inverse = found[t + 1]
                        norm = (tokens[j, at : at + 16, cols].astype(jnp.float32) - mean) * inverse * gain + offset
                        moved = jnp.where(row == 0, before, pltpu.roll(norm, 1, 0))
                        before = norm[15:16]
                        gap = norm - moved
                        to = pl.ds(pl.multiple_of(j * 2 * BLOCK_LEN + at, 16), 16)
                        prev[to, cols] = moved.astype(low)
                        delta[to, cols] = gap.astype(low)
                        for p in range(4):
                            mix[p, to, cols] = (moved + set_ref[2 + p : 3 + p, cols] * gap).astype(low)
                    return carry

                lax.fori_loop(0, width // step, columns, 0)
            return carry

        lax.fori_loop(0, 2, mix_block, 0)

    gathered.wait_passed()

    @pl.when(y != 1)
    def _():
        for one in edges:
            one.start()

    mix_pair(gathered.ring.right)
    x_last.forward()
    z_last.forward()
    mix_pair(y)
    gathered.far_pair()

    @pl.when(y == 1)
    def _():
        for one in edges:
            one.start()

    mix_pair(gathered.ring.far)
    mix_pair(gathered.ring.left)
    prev_out = pltpu.make_async_copy(prev, prev_ref, local.at[3])
    prev_out.start()
    delta_out = pltpu.make_async_copy(delta, delta_ref, local.at[4])
    delta_out.start()
    for ring in (x_last, z_last):
        ring.wait_near()
        ring.wait_far()
    time_out = pltpu.make_async_copy(time, time_ref, local.at[5])
    time_out.start()

    def project(n, carry):
        to = pl.ds(pl.multiple_of(n * 256, 256), 256)
        for p, out in enumerate((r_ref, k_ref, v_ref, g_ref)):
            out[to] = nn(mix[p, to], time[p].reshape(16 * 128, own)).astype(out.dtype)
        return carry

    lax.fori_loop(0, 4, project, 0)
    for one in channel:
        one.wait_recv()
    copy.wait_sent()
    for one in kept + [prev_out, delta_out, time_out]:
        one.wait()


def opening(tokens, time_weights, channel_key, channel_value, channel_gate, vector_block, cid):
    rows, width = tokens.shape
    own = width // 8
    stripe = 2 * (channel_key.shape[1] // 8) + own
    shape = jax.ShapeDtypeStruct
    return pl.pallas_call(
        opening_kernel,
        name="opening",
        cost_estimate=cost(60),
        out_shape=[
            shape((8 * rows, own), low),
            shape((8 * rows, own), low),
            shape((8 * rows, own), low),
            shape((8 * rows, own), jnp.float32),
            shape((16, width), jnp.float32),
            shape((5, 4, 4, 128, own), low),
            shape((8 * rows, width), low),
            shape((8 * rows, width), low),
            shape((128, stripe), low),
        ],
        in_specs=[VMEM] * 6,
        out_specs=[VMEM] * 5 + [HBM] * 4,
        scratch_shapes=[
            pltpu.VMEM((9, rows, width), low),
            pltpu.VMEM((5, 4, 4, 128, own), low),
            pltpu.VMEM((4, 8 * rows, width), low),
            pltpu.VMEM((8 * rows, width), low),
            pltpu.VMEM((8 * rows, width), low),
            pltpu.VMEM((7, 16, 128), low),
            pltpu.VMEM((16, 128), low),
            pltpu.VMEM((16, 16, 128), low),
            pltpu.SemaphoreType.DMA((88,)),
            pltpu.SemaphoreType.DMA((88,)),
            pltpu.SemaphoreType.DMA((6,)),
        ],
        compiler_params=pltpu.CompilerParams(collective_id=cid, has_side_effects=True, vmem_limit_bytes=56 * 2**20),
    )(tokens, time_weights, channel_key, channel_value, channel_gate, vector_block)


class Scatter:
    def __init__(self, copy, p, out, from_sibling, mid, from_left, from_right, end_left, end_right):
        y, self.c, right, left, far = ring_places()
        self.order = (far, right, left, y)
        self.copy, self.p, self.out, self.from_sibling, self.mid = copy, p, out, from_sibling, mid
        self.from_left, self.from_right, self.end_left, self.end_right = from_left, from_right, end_left, end_right
        self.to_sibling, self.to_right, self.to_left = {"core": 1 - self.c}, {"y": right}, {"y": left}
        half = p.shape[1] // 2
        self.first, self.last = pl.ds(0, half), pl.ds(half, half)
        self.near = [None] * 4

    def send(self, src, dst, device):
        one = self.copy(src, dst, device)
        one.start()
        return one

    def share(self, k):
        self.near[k] = self.send(self.p.at[self.order[k] * 2 + 1 - self.c], self.from_sibling.at[k], self.to_sibling)

    def summed(self, k, rows):
        own = self.p[self.order[k] * 2 + self.c, rows].astype(jnp.float32)
        return own + self.from_sibling[k, rows].astype(jnp.float32)

    def far_out(self):
        self.near[0].wait_recv()
        self.mid[0] = self.summed(0, slice(None)).astype(low)
        self.far_right = self.send(self.mid.at[0, self.first], self.from_left, self.to_right)
        self.far_left = self.send(self.mid.at[0, self.last], self.from_right, self.to_left)

    def right_b(self):
        self.near[1].wait_recv()
        self.mid[1, self.last] = self.summed(1, self.last).astype(low)
        self.last_right = self.send(self.mid.at[1, self.last], self.end_left.at[self.last], self.to_right)

    def left_b(self):
        self.near[2].wait_recv()
        self.mid[2, self.first] = self.summed(2, self.first).astype(low)
        self.first_left = self.send(self.mid.at[2, self.first], self.end_right.at[self.first], self.to_left)

    def right_a(self):
        self.far_right.wait_recv()
        value = self.summed(1, self.first) + self.from_left[...].astype(jnp.float32)
        self.mid[1, self.first] = value.astype(low)
        self.first_right = self.send(self.mid.at[1, self.first], self.end_left.at[self.first], self.to_right)

    def left_a(self):
        self.far_left.wait_recv()
        value = self.summed(2, self.last) + self.from_right[...].astype(jnp.float32)
        self.mid[2, self.last] = value.astype(low)
        self.last_left = self.send(self.mid.at[2, self.last], self.end_right.at[self.last], self.to_left)

    def finish(self):
        self.near[3].wait_recv()
        self.last_right.wait_recv()
        self.first_left.wait_recv()
        self.first_right.wait_recv()
        self.last_left.wait_recv()
        from_ring = self.end_left[...].astype(jnp.float32) + self.end_right[...].astype(jnp.float32)
        self.out[...] = self.summed(3, slice(None)) + from_ring


def scatter_scratch(rows, cols):
    return [
        pltpu.VMEM((4, rows, cols), low),
        pltpu.VMEM((3, rows, cols), low),
        pltpu.VMEM((rows // 2, cols), low),
        pltpu.VMEM((rows // 2, cols), low),
        pltpu.VMEM((rows, cols), low),
        pltpu.VMEM((rows, cols), low),
    ]


def group_and_line():
    x = lax.axis_index("x")
    place, member, far, near, far_devices, near_devices = cube_places()
    return x, member, near, near_devices, {"x": lax.rem(x + 1, 4)}, {"x": lax.rem(x + 3, 4)}


class Tokens:
    def __init__(self, copy, slots, member):
        c = lax.axis_index("core")
        half = slots.shape[1] // 2
        self.copy, self.c, self.slots, self.to_sibling = copy, c, slots, {"core": 1 - c}
        self.ring = Ring(copy, "y", lambda at, n: slots.at[at * 2 + c, pl.ds(n * half, half)])
        self.near = copy(slots.at[member], slots.at[member], self.to_sibling)
        self.near.start()

    def pass_on(self, at):
        one = self.copy(self.slots.at[at * 2 + self.c], self.slots.at[at * 2 + self.c], self.to_sibling)
        one.start()
        return one

    def wait_next(self):
        self.ring.wait_near()
        self.passed = [self.pass_on(self.ring.right), self.pass_on(self.ring.left)]

    def wait_passed(self):
        self.near.wait_recv()
        for one in self.passed:
            one.wait_recv()

    def next_pairs(self):
        self.ring.forward()
        self.wait_next()
        self.wait_passed()

    def far_pair(self):
        self.ring.wait_far()
        self.passed.append(self.pass_on(self.ring.far))
        self.passed[-1].wait_recv()

    def copies(self):
        return self.ring.near + [self.ring.far_right, self.ring.far_left, self.near] + self.passed


class Blend:
    def __init__(self, copy, terms, coefficients, delta, p, sums, firsts, to_previous):
        self.terms, self.coefficients, self.delta, self.p, self.sums, self.firsts = terms, coefficients, delta, p, sums, firsts
        self.edge = copy(firsts.at[0], firsts.at[4], to_previous)
        self.row = lax.broadcasted_iota(jnp.int32, (16, p.shape[2]), 0)

    def pair(self, q):
        for s in range(2):
            after = jnp.zeros((1, self.p.shape[2]), jnp.float32)
            for b in (1, 0):

                def slab(t, following):
                    at = s * BLOCK_LEN + (BLOCK_LEN // 16 - 1 - t) * 16
                    rows = pl.ds(pl.multiple_of(b * 2 * BLOCK_LEN + at, 16), 16)
                    gap = self.delta[pl.ds(pl.multiple_of(q * 4 * BLOCK_LEN + b * 2 * BLOCK_LEN + at, 16), 16)]
                    gap = gap.astype(jnp.float32)
                    here, whole = 0.0, 0.0
                    for n, coefficient in enumerate(self.coefficients):
                        term = self.terms[n, rows]
                        here = here + coefficient * term
                        whole = whole + term
                        product = gap * term
                        self.sums[n] += product[:8] + product[8:]
                    behind = whole - here
                    moved = jnp.where(self.row == 15, following, pltpu.roll(behind, 15, 0))
                    self.p[q * 2 + b, pl.ds(pl.multiple_of(at, 16), 16)] = (here + moved).astype(low)
                    return behind[0:1]

                after = lax.fori_loop(0, BLOCK_LEN // 16, slab, after)
            self.firsts[q, s, 0:1, :] = after

        @pl.when(q == 0)
        def _():
            self.edge.start()

    def close(self, q):
        @pl.when(q == 3)
        def _():
            self.edge.wait_recv()

        for s in range(2):
            following = self.firsts[q + 1, s, 0:1, :]
            following = jnp.where(jnp.logical_and(q == 3, lax.axis_index("x") == 3), 0.0, following)
            rows = slice(s * BLOCK_LEN + BLOCK_LEN - 16, (s + 1) * BLOCK_LEN)
            value = self.p[q * 2 + 1, rows].astype(jnp.float32)
            self.p[q * 2 + 1, rows] = (value + jnp.where(self.row == 15, following, 0.0)).astype(low)


def channel_kernel(
    own_ref, hidden_ref, up_ref, w_hbm, set_ref,
    out_ref, grad_ref, sums_ref, dw_ref,
    slots, w, ckey, cgate, delta, rect, hidden, gown, pre, gg, gg_own, gkey, terms, p, value, sums, firsts, dw,
    from_sibling, mid, from_left, from_right, end_left, end_right, send, recv, local,
):
    x, member, near, near_devices, to_next, to_previous = group_and_line()
    y, c, right, left, far = ring_places()
    firsts[0:4] = jnp.zeros_like(firsts[0:4])
    sums[...] = jnp.zeros_like(sums)
    greet(near_devices + [to_next, to_previous])
    copy = Copies(send, recv)
    load = pltpu.make_async_copy(w_hbm, w, local.at[0])
    load.start()
    slots[member] = own_ref[...]
    gathered = Tokens(copy, slots, member)
    wide = rect.shape[1]
    cols = gown.shape[2]
    row = lax.broadcasted_iota(jnp.int32, (16, own_ref.shape[1]), 0)
    edges = [
        copy(slots.at[7, pl.ds(s * BLOCK_LEN + BLOCK_LEN - 16, 16)], slots.at[8, pl.ds(s * BLOCK_LEN + BLOCK_LEN - 16, 16)], to_next)
        for s in range(2)
    ]

    def compute(q):
        @pl.when(q == 0)
        def _():
            for one in edges:
                one.wait_recv()

        for b in range(2):
            j = q * 2 + b
            for s in range(2):
                before = slots[jnp.where(j == 0, 8, j - 1), s * BLOCK_LEN + BLOCK_LEN - 16 : (s + 1) * BLOCK_LEN]
                before = before.astype(jnp.float32)[15:16]
                before = jnp.where(jnp.logical_and(j == 0, x == 0), 0.0, before)

                def slab(t, previous):
                    at = s * BLOCK_LEN + t * 16
                    values = slots[j, pl.ds(pl.multiple_of(at, 16), 16)].astype(jnp.float32)
                    moved = jnp.where(row == 0, previous, pltpu.roll(values, 1, 0))
                    gap = values - moved
                    to = pl.ds(pl.multiple_of(j * 2 * BLOCK_LEN + at, 16), 16)
                    delta[to] = gap.astype(low)
                    ckey[to] = (moved + set_ref[11:12, :] * gap).astype(low)
                    cgate[to] = (moved + set_ref[12:13, :] * gap).astype(low)
                    return values[15:16]

                lax.fori_loop(0, BLOCK_LEN // 16, slab, before)
        rows = pl.ds(pl.multiple_of(q * 256, 256), 256)
        kept = jnp.maximum(nn(ckey[rows], w[:, :wide]), 0.0)
        rect[rows] = kept.astype(low)
        hidden[rows] = (kept * kept).astype(low)
        part = nt(hidden[rows], w[:, wide : 2 * wide]).astype(low)
        early = nn(cgate[rows], w[:, 2 * wide :]).astype(low)
        for b in range(2):
            p[q * 2 + b] = part[b * 128 : (b + 1) * 128]
            gown[q * 2 + b] = early[b * 128 : (b + 1) * 128]

    gates = []

    def give_gate(j):
        one = copy(gown.at[j], pre.at[member], {"y": j // 2, "core": lax.rem(j, 2)})
        one.start()
        gates.append(one)

    buffers = (from_sibling, mid, from_left, from_right, end_left, end_right)
    total = Scatter(copy, p, value, *buffers)
    gathered.next_pairs()

    @pl.when(y != 1)
    def _():
        for one in edges:
            one.start()

    load.wait()
    compute(right)
    total.share(1)
    compute(y)
    total.share(3)
    gathered.far_pair()

    @pl.when(y == 1)
    def _():
        for one in edges:
            one.start()

    copy.wait_sent(edges)
    for turn in range(2):
        give_gate(right * 2 + lax.rem(c + turn, 2))
    give_gate(y * 2 + 1 - c)
    compute(far)
    total.share(0)
    total.right_b()
    compute(left)
    copy.wait_sent(gathered.copies())
    total.share(2)
    total.far_out()
    total.left_b()
    for at in (left, far):
        for turn in range(2):
            give_gate(at * 2 + lax.rem(c + turn, 2))
    pre[member] = gown[member]
    total.right_a()
    total.left_a()
    total.finish()
    for one in gates:
        one.wait_recv()
    copy.wait_sent()

    def gate_block(n, carry):
        at = pl.ds(pl.multiple_of(n * cols, cols), cols)
        gate = jax.nn.sigmoid(pre[n].astype(jnp.float32))
        up = up_ref[:, at].astype(jnp.float32)
        out_ref[:, at] = (hidden_ref[:, at] + gate * value[:, at]).astype(low)
        slots[member, :, at] = (up * gate).astype(low)
        gg_own[n] = (up * value[:, at] * gate * (1.0 - gate)).astype(low)
        return carry

    lax.fori_loop(0, 8, gate_block, 0)

    gathered = Tokens(copy, slots, member)
    gates = [copy(gg_own.at[at], gg.at[member], d) for at, d in zip(near, near_devices)]
    for one in gates:
        one.start()
    gg[member] = gg_own[member]
    blend = Blend(copy, terms, [set_ref[11:12, :], set_ref[12:13, :]], delta, p, sums, firsts, to_previous)

    def compute_back(q):
        rows = pl.ds(pl.multiple_of(q * 256, 256), 256)
        pair = pl.ds(q * 2, 2)
        grad_hidden = nn(slots[pair].reshape(256, slots.shape[2]), w[:, wide : 2 * wide])
        gkey[rows] = (2.0 * grad_hidden * rect[rows].astype(jnp.float32)).astype(low)
        terms[0] = nt(gkey[rows], w[:, :wide])
        terms[1] = nt(gg[pair].reshape(256, cols), w[:, 2 * wide :])
        blend.pair(q)

    total = Scatter(copy, p, grad_ref, *buffers)
    gathered.next_pairs()
    for one in gates:
        one.wait_recv()
    compute_back(y)
    compute_back(right)
    blend.close(y)
    total.share(3)
    compute_back(left)
    blend.close(left)
    total.share(2)
    gathered.far_pair()
    total.left_b()
    compute_back(far)
    blend.close(far)
    total.share(0)
    blend.close(right)
    total.share(1)
    total.far_out()
    total.right_b()

    def give(block, slot):
        at = pl.ds(pl.multiple_of(block * 256, 256), 256)
        return pltpu.make_async_copy(dw.at[slot], dw_ref.at[at], local.at[1 + slot])

    def weight_blocks(n, carry):
        for slot in range(2):
            block = n * 2 + slot
            at = pl.ds(pl.multiple_of(block * 256, 256), 256)

            @pl.when(n > 0)
            def _():
                give(block - 2, slot).wait()

            dw[slot, :, :wide] = tn(ckey[:, at], gkey[...]).astype(low)
            dw[slot, :, wide : 2 * wide] = tn(slots[0:8, :, at].reshape(8 * 128, 256), hidden[...]).astype(low)
            dw[slot, :, 2 * wide :] = tn(cgate[:, at], gg[...].reshape(8 * 128, cols)).astype(low)
            give(block, slot).start()
        return carry

    lax.fori_loop(0, 2, weight_blocks, 0)
    total.right_a()
    total.left_a()
    lax.fori_loop(2, 4, weight_blocks, 0)
    for n in range(2):
        sums_ref[n : n + 1, :] = jnp.sum(sums[n], axis=0, keepdims=True)
    sums_ref[2:8, :] = jnp.zeros((6, sums_ref.shape[1]), jnp.float32)
    total.finish()
    copy.wait_sent()
    for slot in range(2):
        give(6 + slot, slot).wait()


def channel(own, hidden_one, upstream, weights, settings, cid):
    rows, width = own.shape
    cols = width // 8
    wide = (weights.shape[1] - cols) // 2
    shape = jax.ShapeDtypeStruct
    big = pltpu.VMEM((8 * rows, width), low)
    mid = pltpu.VMEM((8 * rows, wide), low)
    small = pltpu.VMEM((8, rows, cols), low)
    return pl.pallas_call(
        channel_kernel,
        name="channel",
        cost_estimate=cost(120),
        out_shape=[
            shape((rows, width), low),
            shape((rows, width), jnp.float32),
            shape((8, width), jnp.float32),
            shape(weights.shape, low),
        ],
        in_specs=[VMEM] * 3 + [HBM, VMEM],
        out_specs=[VMEM] * 3 + [HBM],
        scratch_shapes=[
            pltpu.VMEM((9, rows, width), low),
            pltpu.VMEM(weights.shape, low),
            big,
            big,
            big,
            mid,
            mid,
            small,
            small,
            small,
            small,
            mid,
            pltpu.VMEM((2, 256, width), jnp.float32),
            pltpu.VMEM((8, rows, width), low),
            pltpu.VMEM((rows, width), jnp.float32),
            pltpu.VMEM((2, 8, width), jnp.float32),
            pltpu.VMEM((5, 2, 8, width), jnp.float32),
            pltpu.VMEM((2, 256, weights.shape[1]), low),
            *scatter_scratch(rows, width),
            pltpu.SemaphoreType.DMA((70,)),
            pltpu.SemaphoreType.DMA((70,)),
            pltpu.SemaphoreType.DMA((3,)),
        ],
        compiler_params=pltpu.CompilerParams(collective_id=cid, has_side_effects=True, vmem_limit_bytes=59 * 2**20),
    )(own, hidden_one, upstream, weights, settings)


def middle_kernel(
    second_ref, hidden_ref, up_ref, set_ref, column_ref, params_ref,
    g_ref, scaled_ref, inverse_ref, r_ref, k_ref, v_ref, w_ref, in_ref, time_hbm, prev_hbm, delta_hbm, gated_hbm,
    upper_ref, proj_ref, vec_ref, sums_ref, dw_ref,
    time, prev, delta, gated, out, out_all, p, gg, dw, norm_sums, part_k, part_v, suffix, total, slots, sums,
    from_sibling, mid, from_left, from_right, end_left, end_right, send, recv, local,
):
    x, member, near, near_devices, _, _ = group_and_line()
    y, c, right, left, far = ring_places()
    greet(near_devices + [{"x": lax.rem(x + n, 4)} for n in range(1, 4)])
    copy = Copies(send, recv)
    cols = g_ref.shape[1]
    loads = [
        pltpu.make_async_copy(src, dst, local.at[n])
        for n, (src, dst) in enumerate(
            ((time_hbm.at[3:5], time), (gated_hbm, gated), (prev_hbm, prev), (delta_hbm, delta))
        )
    ]
    for one in loads:
        one.start()

    norm_sums[...] = jnp.zeros_like(norm_sums)

    def norm_rows(t, carry):
        rows = pl.ds(pl.multiple_of(t * 16, 16), 16)
        values = hidden_ref[rows]
        center = values - jnp.mean(values, axis=-1, keepdims=True)
        inverse = lax.rsqrt(jnp.mean(center * center, axis=-1, keepdims=True) + epsilon)
        unit = center * inverse
        grad = second_ref[rows]
        product = grad * unit
        norm_sums[0] += product[:8] + product[8:]
        norm_sums[1] += grad[:8] + grad[8:]
        inner = grad * set_ref[9:10, :]
        mean = jnp.mean(inner, axis=-1, keepdims=True)
        along = jnp.mean(inner * unit, axis=-1, keepdims=True)
        upper = up_ref[rows].astype(jnp.float32) + inverse * (inner - mean - unit * along)
        upper_ref[rows] = upper
        for n in range(8):
            out[n, rows] = upper[:, n * cols : (n + 1) * cols].astype(low)
        return carry

    lax.fori_loop(0, 8, norm_rows, 0)
    given = [copy(out.at[at], out_all.at[member], d) for at, d in zip(near, near_devices)]
    for one in given:
        one.start()
    out_all[member] = out[member]
    for n in range(2):
        vec_ref[n : n + 1, :] = jnp.sum(norm_sums[n], axis=0, keepdims=True)
    vec_ref[3:8, :] = jnp.zeros((5, vec_ref.shape[1]), jnp.float32)
    sums[...] = jnp.zeros_like(sums)
    for one in loads:
        one.wait()
    for one in given:
        one.wait_recv()

    def through(q):
        for b in range(2):
            m = q * 2 + b
            rows = pl.ds(pl.multiple_of(m * cols, cols), cols)
            p[m] = nt(out_all[...].reshape(8 * 128, cols), time[1, rows]).astype(low)

    def out_block(m, carry):
        rows = pl.ds(pl.multiple_of(m * cols, cols), cols)
        dw[rows, cols : 2 * cols] = tn(gated[m], out_all[...].reshape(8 * 128, cols)).astype(low)
        return carry

    total_gg = Scatter(copy, p, gg, from_sibling, mid, from_left, from_right, end_left, end_right)
    through(far)
    total_gg.share(0)
    through(right)
    total_gg.share(1)
    through(left)
    total_gg.share(2)
    total_gg.far_out()
    total_gg.right_b()
    total_gg.left_b()
    through(y)
    total_gg.share(3)
    lax.fori_loop(0, 4, out_block, 0)
    total_gg.right_a()
    total_gg.left_a()
    lax.fori_loop(4, 8, out_block, 0)
    total_gg.finish()

    log_row, bonus, gain, bias = [params_ref[n : n + 1, :] for n in range(4)]
    mask, eye, enter, leave, same = head_tables(log_row)
    block_decay = jnp.exp(BLOCK_LEN * log_row)
    ones = jnp.where(same, 1.0, 0.0).astype(low)

    def first(m, carry):
        for s in range(2):
            rows = block_rows(m, s)
            gate, grad, scaled = g_ref[rows], gg[rows], scaled_ref[rows]
            sigma = jax.nn.sigmoid(gate)
            grad_normed = grad * gate * sigma
            proj_ref[3, rows] = (grad * (scaled * gain + bias) * sigma * (1.0 + gate * (1.0 - sigma))).astype(low)
            inner = grad_normed * gain
            wide = inverse_ref[rows] * (inner - head_mean(inner, same) - scaled * head_mean(inner * scaled, same))
            grad_wkv = wide.astype(low)
            r, k, v = r_ref[rows], k_ref[rows], v_ref[rows]
            r_wide, k_wide = r.astype(jnp.float32), k.astype(jnp.float32)
            grad_weights = nt(grad_wkv, expand(v, same)).astype(low).astype(jnp.float32)
            masked = (grad_weights * mask).astype(low)
            own = nn(jnp.where(eye, grad_weights, 0.0).astype(low), ones)
            grad_r = nn(masked, expand(k, same)) + own * bonus * k_wide
            grad_r = grad_r + nt(grad_wkv, expand(in_ref[m * 2 + s], same)) * enter
            proj_ref[0, rows] = grad_r.astype(low)
            part_k[rows] = compress(tn(masked, r), same) + own * bonus * r_wide
            part_v[rows] = compress(tn(w_ref[rows], grad_wkv), same)
            suffix[m * 2 + s] = compress(tn((r_wide * enter).astype(low), grad_wkv), same)
            sums[0] += own * r_wide * k_wide
            sums[1] += grad_normed * scaled
            sums[2] += grad_normed
        return carry

    lax.fori_loop(0, 8, first, 0)

    def chain(n, states):
        m = 7 - n
        after = []
        for s in range(2):
            here = suffix[m * 2 + s]
            suffix[m * 2 + s] = states[s]
            after.append(states[s] * block_decay + here)
        return tuple(after)

    zero = jnp.zeros(enter.shape, jnp.float32)
    states = lax.fori_loop(0, 8, chain, (zero, zero))
    for s in range(2):
        total[s] = states[s]
    line = start_line(total, slots, send.at[pl.ds(40, 3)], recv.at[pl.ds(40, 3)])

    def gate_block(n, carry):
        rows = pl.ds(pl.multiple_of(n * cols, cols), cols)
        by_delta = tn(delta[:, rows], proj_ref[3])
        column = column_ref[rows]
        grads = tn(prev[:, rows], proj_ref[3]) + column[:, 5:6] * by_delta
        dw[rows, :cols] = grads.astype(low)
        product = (time[0, rows].astype(jnp.float32) * by_delta).astype(low)
        vec_ref[2:3, rows] = nt(jnp.ones((8, cols), low), product)[0:1]
        return carry

    lax.fori_loop(0, 8, gate_block, 0)
    give = pltpu.make_async_copy(dw, dw_ref, local.at[4])
    give.start()
    for one in line:
        one.wait()
    x_place = lax.axis_index("x")
    leaving = [zero, zero]
    span_decay = jnp.exp(8.0 * BLOCK_LEN * log_row)
    for x in (3, 2, 1):
        for s in range(2):
            leaving[s] = jnp.where(x > x_place, leaving[s] * span_decay + slots[x, s], leaving[s])
    for s in range(2):
        total[s] = leaving[s]

    def second(m, carry):
        power = jnp.exp(((7 - m) * BLOCK_LEN).astype(jnp.float32) * log_row)
        for s in range(2):
            rows = block_rows(m, s)
            state = expand((suffix[m * 2 + s] + power * total[s]).astype(low), same)
            key_leave = (k_ref[rows].astype(jnp.float32) * leave).astype(low)
            proj_ref[1, rows] = (part_k[rows] + nt(v_ref[rows], state) * leave).astype(low)
            proj_ref[2, rows] = (part_v[rows] + nn(key_leave, state)).astype(low)
        return carry

    lax.fori_loop(0, 8, second, 0)


    for n in range(3):
        sums_ref[n : n + 1, :] = jnp.sum(sums[n], axis=0, keepdims=True)
    sums_ref[3:8, :] = jnp.zeros((5, cols), jnp.float32)
    copy.wait_sent()
    give.wait()


def middle(second, hidden, up, settings, columns, params, g, scaled, inverse, r, k, v, w, states, time, prev, delta, gated, cid):
    rows, width = second.shape
    cols = g.shape[1]
    tall = pltpu.VMEM((8 * rows, cols), jnp.float32)
    shape = jax.ShapeDtypeStruct
    return pl.pallas_call(
        middle_kernel,
        name="middle",
        out_shape=[
            shape((rows, width), jnp.float32),
            shape((4, 8 * rows, cols), low),
            shape((8, width), jnp.float32),
            shape((8, cols), jnp.float32),
            shape((width, 2 * cols), low),
        ],
        in_specs=[VMEM] * 14 + [HBM] * 4,
        out_specs=[VMEM] * 4 + [HBM],
        scratch_shapes=[
            pltpu.VMEM((2, width, cols), low),
            pltpu.VMEM(prev.shape, low),
            pltpu.VMEM(delta.shape, low),
            pltpu.VMEM(gated.shape, low),
            pltpu.VMEM((8, rows, cols), low),
            pltpu.VMEM((8, rows, cols), low),
            pltpu.VMEM((8, 8 * rows, cols), low),
            tall,
            pltpu.VMEM((width, 2 * cols), low),
            pltpu.VMEM((2, 8, width), jnp.float32),
            tall,
            tall,
            pltpu.VMEM((16, BLOCK_LEN, cols), jnp.float32),
            pltpu.VMEM((2, BLOCK_LEN, cols), jnp.float32),
            pltpu.VMEM((4, 2, BLOCK_LEN, cols), jnp.float32),
            pltpu.VMEM((3, BLOCK_LEN, cols), jnp.float32),
            *scatter_scratch(8 * rows, cols),
            pltpu.SemaphoreType.DMA((43,)),
            pltpu.SemaphoreType.DMA((43,)),
            pltpu.SemaphoreType.DMA((5,)),
        ],
        compiler_params=pltpu.CompilerParams(collective_id=cid, has_side_effects=True, vmem_limit_bytes=58 * 2**20),
    )(second, hidden, up, settings, columns, params, g, scaled, inverse, r, k, v, w, states, time, prev, delta, gated)


class RingScatter:
    def __init__(self, copy, axis, part, halves, bufs):
        me = lax.axis_index(axis)
        right, left, self.far = [lax.rem(me + k, 4) for k in (1, 3, 2)]
        self.me, self.right, self.left, self.part, self.halves, self.copy = me, right, left, part, halves, copy
        self.to_right, self.to_left = {axis: right}, {axis: left}
        self.from_left, self.from_right, self.end_left, self.end_right = bufs

    def send(self, src, dst, device):
        one = self.copy(src, dst, device)
        one.start()
        return one

    def far_out(self):
        first, last = self.halves
        self.far_right = self.send(self.part(self.far).at[first], self.from_left, self.to_right)
        self.far_left = self.send(self.part(self.far).at[last], self.from_right, self.to_left)

    def near_out(self):
        first, last = self.halves
        self.last_right = self.send(self.part(self.right).at[last], self.end_left.at[last], self.to_right)
        self.first_left = self.send(self.part(self.left).at[first], self.end_right.at[first], self.to_left)

    def pass_on(self):
        first, last = self.halves
        self.far_right.wait_recv()
        here = self.part(self.right).at[first]
        here[...] = (here[...].astype(jnp.float32) + self.from_left[...].astype(jnp.float32)).astype(low)
        self.first_right = self.send(here, self.end_left.at[first], self.to_right)
        self.far_left.wait_recv()
        here = self.part(self.left).at[last]
        here[...] = (here[...].astype(jnp.float32) + self.from_right[...].astype(jnp.float32)).astype(low)
        self.last_left = self.send(here, self.end_right.at[last], self.to_left)

    def finish(self, out):
        for one in (self.last_right, self.first_left, self.first_right, self.last_left):
            one.wait_recv()
        value = self.part(self.me)[...].astype(jnp.float32) + self.end_left[...].astype(jnp.float32)
        out[...] = (value + self.end_right[...].astype(jnp.float32)).astype(low)


def closing_kernel(
    grad_ref, early_hbm, time_hbm, prev_hbm, delta_hbm, set_ref, column_ref, tok_ref, upper_ref, vec_ref,
    token_ref, weight_ref, total_ref,
    time, scaled, prev, delta, early, terms, p, firsts, one_dw, other_dw, one_sum, other_sum, stripe, gathered, parts,
    one_a, one_b, one_c, one_d, other_a, other_b, other_c, other_d,
    one_e, one_f, one_g, one_h, other_e, other_f, other_g, other_h,
    early_a, early_b, early_c, early_d, early_e, early_f, early_g, early_h,
    early_i, early_j, early_k, early_l, early_m, early_n, early_o, early_p, early_one, early_other, vec_far, vec_near, vec_stripe, first_grad, norm_sums,
    from_sibling, mid, from_left, from_right, end_left, end_right, send, recv, local,
):
    place, member, far_places, near_members, far_devices, near_devices = cube_places()
    x = lax.axis_index("x")
    y, c, right, left, far = ring_places()
    to_previous = {"x": lax.rem(x + 3, 4)}
    firsts[0:4] = jnp.zeros_like(firsts[0:4])
    greet(far_devices + near_devices)
    copy = Copies(send, recv)
    cols = grad_ref.shape[2]
    loads = [
        pltpu.make_async_copy(src, dst, local.at[n])
        for n, (src, dst) in enumerate(
            ((early_hbm, early), (prev_hbm, prev), (delta_hbm, delta), (time_hbm.at[0:4], time))
        )
    ]
    for one in loads:
        one.start()
    slots = (pl.ds(0, 2), pl.ds(2, 2))
    halves = (pl.ds(0, 64), pl.ds(64, 64))
    side = early.shape[3] // 2
    loads[0].wait()
    early_z = RingScatter(copy, "z", lambda at: early.at[at, :, :, 0:side], slots, (early_a, early_b, early_c, early_d))
    early_x = RingScatter(
        copy, "x", lambda at: early.at[:, at, :, side : 2 * side], slots, (early_e, early_f, early_g, early_h)
    )
    for ring in (early_z, early_x):
        ring.far_out()
        ring.near_out()
    for one in loads[1:]:
        one.wait()

    ones = jnp.ones((8, cols), low)

    def weight_block(at):
        def part(h, carry):
            block = at * 2 + h
            rows = pl.ds(pl.multiple_of(block * 256, 256), 256)
            prev_block, delta_block = prev[:, rows].T, delta[:, rows].T
            column = column_ref[rows]
            scaled[3, rows] = (column[:, 5:6] * time[3, rows].astype(jnp.float32)).astype(low)
            grads = []
            for n in range(3):
                by_delta = nn(delta_block, grad_ref[n])
                factor = column[:, 2 + n : 3 + n]
                grads.append((nn(prev_block, grad_ref[n]) + factor * by_delta).astype(low))
                weight = time[n, rows].astype(jnp.float32)
                scaled[n, rows] = (factor * weight).astype(low)
                parts[2 + n : 3 + n, rows] = nt(ones, (weight * by_delta).astype(low))[0:1]
            whole = jnp.concatenate(grads, axis=1)
            half = whole.shape[1] // 2
            for k in range(2):
                one_dw[at, h * 2 + k] = whole[k * 128 : (k + 1) * 128, :half]
                other_dw[at, h * 2 + k] = whole[k * 128 : (k + 1) * 128, half:]
            return carry

        lax.fori_loop(0, 2, part, 0)

    parts[...] = vec_ref[...]
    z_first = RingScatter(copy, "z", lambda at: one_dw.at[at], slots, (one_a, one_b, one_c, one_d))
    x_first = RingScatter(copy, "x", lambda at: other_dw.at[:, at], slots, (other_a, other_b, other_c, other_d))

    row = lax.broadcasted_iota(jnp.int32, (16, p.shape[2]), 0)
    edge = copy(firsts.at[0], firsts.at[4], to_previous)

    def compute(q):
        rows = pl.ds(pl.multiple_of(q * 256, 256), 256)
        whole, here = 0.0, 0.0
        for n in range(4):
            whole = whole + nt(grad_ref[n, rows], time[n])
            here = here + nt(grad_ref[n, rows], scaled[n])
        terms[0] = here
        terms[1] = whole - here
        for s in range(2):
            after = jnp.zeros((1, p.shape[2]), jnp.float32)
            for b in (1, 0):

                def slab(t, following):
                    at = s * BLOCK_LEN + (BLOCK_LEN // 16 - 1 - t) * 16
                    rows = pl.ds(pl.multiple_of(b * 2 * BLOCK_LEN + at, 16), 16)
                    behind = terms[1, rows]
                    moved = jnp.where(row == 15, following, pltpu.roll(behind, 15, 0))
                    p[q * 2 + b, pl.ds(pl.multiple_of(at, 16), 16)] = (terms[0, rows] + moved).astype(low)
                    return behind[0:1]

                after = lax.fori_loop(0, BLOCK_LEN // 16, slab, after)
            firsts[q, s, 0:1, :] = after

        @pl.when(q == 0)
        def _():
            edge.start()

    def close(q):
        @pl.when(q == 3)
        def _():
            edge.wait_recv()

        for s in range(2):
            following = firsts[q + 1, s, 0:1, :]
            following = jnp.where(jnp.logical_and(q == 3, x == 3), 0.0, following)
            rows = slice(s * BLOCK_LEN + BLOCK_LEN - 16, (s + 1) * BLOCK_LEN)
            value = p[q * 2 + 1, rows].astype(jnp.float32)
            p[q * 2 + 1, rows] = (value + jnp.where(row == 15, following, 0.0)).astype(low)

    total = Scatter(copy, p, first_grad, from_sibling, mid, from_left, from_right, end_left, end_right)
    weight_block(z_first.far)
    z_first.far_out()
    early_z.pass_on()
    early_x.pass_on()
    weight_block(z_first.right)
    weight_block(z_first.left)
    z_first.near_out()
    weight_block(z_first.me)
    x_first.far_out()
    x_first.near_out()
    compute(left)
    z_first.pass_on()
    early_z.finish(early_one)
    early_x.finish(early_other)
    early_last_x = RingScatter(copy, "x", lambda at: early_one.at[at], halves, (early_i, early_j, early_k, early_l))
    early_last_z = RingScatter(copy, "z", lambda at: early_other.at[at], halves, (early_m, early_n, early_o, early_p))
    for ring in (early_last_x, early_last_z):
        ring.far_out()
        ring.near_out()
    compute(far)
    close(far)
    total.share(0)
    x_first.pass_on()
    compute(right)
    total.far_out()
    close(right)
    total.share(1)
    total.right_b()
    early_last_x.pass_on()
    early_last_z.pass_on()
    z_first.finish(one_sum)
    x_last = RingScatter(copy, "x", lambda at: one_sum.at[at], halves, (one_e, one_f, one_g, one_h))
    x_last.far_out()
    x_last.near_out()
    compute(y)
    close(left)
    total.share(2)
    close(y)
    total.share(3)
    total.left_b()
    total.right_a()
    total.left_a()
    x_first.finish(other_sum)
    z_last = RingScatter(copy, "z", lambda at: other_sum.at[at], halves, (other_e, other_f, other_g, other_h))
    z_last.far_out()
    z_last.near_out()
    x_last.pass_on()
    z_last.pass_on()
    early_last_x.finish(stripe.at[:, 3 * cols : 3 * cols + side])
    early_last_z.finish(stripe.at[:, 3 * cols + side : 3 * cols + 2 * side])
    half = one_sum.shape[2]
    x_last.finish(stripe.at[:, 0:half])
    z_last.finish(stripe.at[:, half : 2 * half])
    given = [
        copy(stripe.at[pl.ds(pl.multiple_of(at * 16, 16), 16)], gathered.at[member], d)
        for at, d in zip(near_members, near_devices)
    ]
    for one in given:
        one.start()
    gathered[member] = stripe[pl.ds(pl.multiple_of(member * 16, 16), 16)]
    total.finish()

    norm_sums[...] = jnp.zeros_like(norm_sums)

    def norm_rows(t, carry):
        rows = pl.ds(pl.multiple_of(t * 16, 16), 16)
        values = tok_ref[rows].astype(jnp.float32)
        center = values - jnp.mean(values, axis=-1, keepdims=True)
        inverse = lax.rsqrt(jnp.mean(center * center, axis=-1, keepdims=True) + epsilon)
        unit = center * inverse
        grad = first_grad[rows]
        product = grad * unit
        norm_sums[0] += product[:8] + product[8:]
        norm_sums[1] += grad[:8] + grad[8:]
        inner = grad * set_ref[0:1, :]
        mean = jnp.mean(inner, axis=-1, keepdims=True)
        along = jnp.mean(inner * unit, axis=-1, keepdims=True)
        token_ref[rows] = (upper_ref[rows] + inverse * (inner - mean - unit * along)).astype(low)
        return carry

    lax.fori_loop(0, 8, norm_rows, 0)
    for n in range(2):
        parts[n : n + 1, :] = jnp.sum(norm_sums[n], axis=0, keepdims=True)
    vec_first = [
        copy(parts.at[:, pl.ds(pl.multiple_of(at * 128, 128), 128)], vec_far.at[n], d)
        for n, (at, d) in enumerate(zip(far_places, far_devices))
    ]
    for one in vec_first:
        one.start()
    sum_all = parts[:, pl.ds(pl.multiple_of(place * 128, 128), 128)]
    for n, one in enumerate(vec_first):
        one.wait_recv()
        sum_all = sum_all + vec_far[n]
    vec_stripe[...] = sum_all
    vec_last = [copy(vec_stripe, vec_near.at[n], d) for n, d in enumerate(near_devices)]
    for one in vec_last:
        one.start()
    for one in given:
        one.wait_recv()
    for m in range(8):
        for n in range(5):
            weight_ref[n, :, m * cols : (m + 1) * cols] = gathered[m, :, n * cols : (n + 1) * cols].astype(jnp.float32)
    for n, one in enumerate(vec_last):
        one.wait_recv()
        sum_all = sum_all + vec_near[n]
    total_ref[...] = sum_all
    copy.wait_sent()


def closing(grads, early, time, prev, delta, settings, columns, tokens, upper, vec, cid):
    _, width, cols = time.shape
    rows = delta.shape[0] // 8
    half, side = 3 * cols // 2, cols
    early = early.reshape(4, 4, 128, 2 * cols)
    shape = jax.ShapeDtypeStruct
    wide = [pltpu.VMEM((2, 128, half), low)] * 2 + [pltpu.VMEM((4, 128, half), low)] * 2
    thin = [pltpu.VMEM((64, half), low)] * 2 + [pltpu.VMEM((128, half), low)] * 2
    early_wide = [pltpu.VMEM((2, 128, side), low)] * 2 + [pltpu.VMEM((4, 128, side), low)] * 2
    early_thin = [pltpu.VMEM((64, side), low)] * 2 + [pltpu.VMEM((128, side), low)] * 2
    early_sum = pltpu.VMEM((4, 128, side), low)
    return pl.pallas_call(
        closing_kernel,
        name="closing",
        out_shape=[
            shape((rows, width), low),
            shape((5, 16, width), jnp.float32),
            shape((16, 128), jnp.float32),
        ],
        in_specs=[VMEM, HBM, HBM, HBM, HBM, VMEM, VMEM, VMEM, VMEM, VMEM],
        out_specs=[VMEM] * 3,
        scratch_shapes=[
            pltpu.VMEM((4, width, cols), low),
            pltpu.VMEM((4, width, cols), low),
            pltpu.VMEM(delta.shape, low),
            pltpu.VMEM(delta.shape, low),
            pltpu.VMEM(early.shape, low),
            pltpu.VMEM((2, 256, width), jnp.float32),
            pltpu.VMEM((8, rows, width), low),
            pltpu.VMEM((5, 2, 8, width), jnp.float32),
            pltpu.VMEM((4, 4, 128, half), low),
            pltpu.VMEM((4, 4, 128, half), low),
            pltpu.VMEM((4, 128, half), low),
            pltpu.VMEM((4, 128, half), low),
            pltpu.VMEM((128, 5 * cols), low),
            pltpu.VMEM((8, 16, 5 * cols), low),
            pltpu.VMEM((16, width), jnp.float32),
            *wide,
            *wide,
            *thin,
            *thin,
            *early_wide,
            *early_wide,
            *early_thin,
            *early_thin,
            early_sum,
            early_sum,
            pltpu.VMEM((15, 16, 128), jnp.float32),
            pltpu.VMEM((7, 16, 128), jnp.float32),
            pltpu.VMEM((16, 128), jnp.float32),
            pltpu.VMEM((rows, width), jnp.float32),
            pltpu.VMEM((2, 8, width), jnp.float32),
            *scatter_scratch(rows, width),
            pltpu.SemaphoreType.DMA((104,)),
            pltpu.SemaphoreType.DMA((104,)),
            pltpu.SemaphoreType.DMA((4,)),
        ],
        compiler_params=pltpu.CompilerParams(collective_id=cid, has_side_effects=True, vmem_limit_bytes=59 * 2**20),
    )(grads, early, time, prev, delta, settings, columns, tokens, upper, vec)


def body(tokens, time_weights, channel_key, channel_value, channel_gate, vectors, head_decay, lengths, cotangent):
    groups, span, width = tokens.shape
    features = channel_key.shape[1]
    local_rows = channel_key.shape[0]
    members = lax.axis_size(GROUP)
    member = lax.axis_index(GROUP)
    x_size, x_place = lax.axis_size("x"), lax.axis_index("x")
    heads = head_decay.shape[0] // members
    head_width = width // head_decay.shape[0]
    own = width // members
    own_features = features // members
    row_count = groups * span
    all_rows = members * row_count
    stripe = members * local_rows

    vector_rows = vectors.shape[0]
    vector_block = lax.dynamic_update_slice(jnp.zeros((16, stripe), low), vectors, (0, member * local_rows))
    recv, key, value, gate_pre, settings, time_full, first_prev, first_delta, channel_part = opening(
        tokens.reshape(row_count, width), time_weights, channel_key, channel_value, channel_gate, vector_block, 1
    )
    time_full = time_full.reshape(5, width, own)
    channel_full = lax.all_gather(channel_part, ROWS, axis=0, tiled=True)
    own_settings = lax.dynamic_slice_in_dim(settings, member * own, own, axis=1)

    log_decay = jnp.log(lax.dynamic_slice_in_dim(head_decay, member * heads, heads))
    params = jnp.concatenate(
        [jnp.repeat(log_decay, head_width)[None], own_settings[6:9], jnp.zeros((4, own), jnp.float32)]
    )
    weights, wkv_scaled, wkv_inverse, incoming, hidden_one, second, gated_all = recurrence(
        recv, key, value, gate_pre, params, tokens.reshape(row_count, width), settings, time_full, 3
    )

    offsets = lax.axis_index(SEQ) * span + jnp.arange(span, dtype=jnp.int32)
    upstream = jnp.where((offsets[None, :] < lengths[:, None])[:, :, None], cotangent, jnp.zeros((), low))
    upstream = upstream.reshape(row_count, width)
    layer_out, grad_second, channel_sums, channel_term = channel(
        second, hidden_one, upstream, channel_full, settings, 7
    )
    layer_out = layer_out.reshape(groups, span, width)
    mix_key_grad, mix_gate_grad = channel_sums[0], channel_sums[1]
    channel_sum = lax.psum_scatter(channel_term, ROWS, scatter_dimension=0, tiled=True)
    upper, grad_proj, middle_sums, own_sums, early_term = middle(
        grad_second,
        hidden_one,
        upstream,
        settings,
        settings.T,
        params,
        gate_pre,
        wkv_scaled,
        wkv_inverse,
        recv,
        key,
        value,
        weights,
        incoming,
        time_full,
        first_prev,
        first_delta,
        gated_all,
        4,
    )
    bonus_grad, norm_gain_grad, norm_bias_grad = own_sums[0], own_sums[1], own_sums[2]
    second_gain_grad, second_bias_grad = middle_sums[0], middle_sums[1]
    def spread_own(row):
        return lax.dynamic_update_slice_in_dim(jnp.zeros((width,), jnp.float32), row, member * own, axis=0)

    nothing = jnp.zeros((width,), jnp.float32)
    vector_term = jnp.stack(
        [nothing] * 5
        + [middle_sums[2]]
        + [
            spread_own(bonus_grad),
            spread_own(norm_gain_grad),
            spread_own(norm_bias_grad),
            second_gain_grad,
            second_bias_grad,
            mix_key_grad,
            mix_gate_grad,
        ]
        + [nothing] * 3
    )
    token_grad, time_grads, vector_sum = closing(
        grad_proj,
        early_term,
        time_full,
        first_prev,
        first_delta,
        settings,
        settings.T,
        tokens.reshape(row_count, width),
        upper,
        vector_term,
        9,
    )
    token_grad = token_grad.reshape(groups, span, width)
    channel_sum, vector_sum = lax.optimization_barrier((channel_sum, vector_sum))
    channel_sum = lax.all_to_all(
        channel_sum.reshape(members, local_rows, 2 * own_features + own), GROUP, split_axis=0, concat_axis=0, tiled=True
    )
    channel_sum = jnp.swapaxes(channel_sum, 0, 1).astype(jnp.float32)
    key_grad = channel_sum[:, :, :own_features].reshape(local_rows, features)
    value_grad = channel_sum[:, :, own_features : 2 * own_features].reshape(local_rows, features)
    gate_grad = channel_sum[:, :, 2 * own_features :].reshape(local_rows, width)
    vector_sum = lax.dynamic_slice(vector_sum, (0, member * local_rows), (vector_rows, local_rows))
    return layer_out, token_grad, time_grads, key_grad, value_grad, gate_grad, vector_sum


def solution(mesh):
    batch, seq = mesh.devices.shape
    side = 4
    fine = Mesh(mesh.devices.reshape(batch, side, seq // (2 * side), 2), ALL)
    return jax.shard_map(
        body,
        mesh=fine,
        in_specs=(
            P("z", SEQ, None),
            P(None, ALL, None),
            P(ALL, None),
            P(ALL, None),
            P(ALL, None),
            P(None, ALL),
            P(),
            P("z"),
            P("z", SEQ, None),
        ),
        out_specs=(
            P("z", SEQ, None),
            P("z", SEQ, None),
            P(None, ALL, None),
            P(ALL, None),
            P(ALL, None),
            P(ALL, None),
            P(None, ALL),
        ),
        check_vma=False,
    )
```

time: 2880 us -> 458 us (0.16)
  waiting for transfers between devices: 2000 us -> 11.2 us
  Pallas kernels: 0 us -> 394 us
  matrix products: 244 us -> 0 us
  local copies, waits for them, and re-layouts: 241 us -> 28.1 us
  other arithmetic: 183 us -> 1.14 us
  blocking collectives: 166 us -> 0 us
    reduce_scatter x2 -> x1, waiting for transfers between devices: 1250 us -> 0.02 us  [body(): lax.psum_scatter(channel_term, ROWS, scatter_dimension=0, tiled=True)]
    unnamed x10 -> x2, waiting for transfers between devices: 444 us -> 0.03 us
    pallas_call x0 -> x5, Pallas kernels: none -> 394 us  [the longest x1 133 us: channel(): pl.pallas_call(channel_kernel, name='channel', cost_estimate=cost(120), o...]
    all_gather x6 -> x1, waiting for transfers between devices: 307 us -> 3.09 us  [body(): channel_full = lax.all_gather(channel_part, ROWS, axis=0, tiled=True)]
    dot_general x24 -> x0, matrix products: 244 us -> none  [the longest x4 48.9 us: matmul_right(): lax.dot_general(left_mat, right_mat, (((1,), (1,)), ((), ())), preferred_...]
    select_n x66 -> x1, other arithmetic: 143 us -> 0.9 us  [body(): jnp.where((offsets[None, :] < lengths[:, None])[:, :, None], cotangent, j...]
    unnamed x2 -> x0, blocking collectives: 126 us -> none
    reshape x6 -> x3, local copies, waits for them, and re-layouts: 121 us -> 2.26 us  [the longest x1 0.8 us: body(): key_grad = channel_sum[:, :, :own_features].reshape(local_rows, features)]
  transfers between devices with their start and end apart: 13 -> 3, of which waited for: 9 -> 2; matrix products, arithmetic and copies ran while one was open for 15% -> 3% of each run, Pallas kernels for 0% -> 43%
where the time goes in v2:
time: 458 us; the launch traced here: 453 us
  Pallas kernels  394 us (86%)
  local copies, waits for them, and re-layouts  28.1 us (6%)
  between operations  14.7 us (3%)
  waiting for transfers between devices  11.2 us (2%)
    pallas_call x1, Pallas kernels, channel(): pl.pallas_call(channel_kernel, name='channel', cost_estimate=cost(120), o...  133 us
    pallas_call x1, Pallas kernels, closing(): pl.pallas_call(closing_kernel, name='closing', out_shape=[shape((rows, wi...  78.2 us
    pallas_call x1, Pallas kernels, opening(): pl.pallas_call(opening_kernel, name='opening', cost_estimate=cost(60), ou...  64.2 us
    pallas_call x1, Pallas kernels, middle(): pl.pallas_call(middle_kernel, name='middle', out_shape=[shape((rows, widt...  60.6 us
    pallas_call x1, Pallas kernels, recurrence(): pl.pallas_call(recurrence_kernel, name='recurrence', cost_estimate=cost(5...  57.7 us
    unnamed x41, local copies, waits for them, and re-layouts  13.5 us
  transfers between devices with their start and end apart: 3, of which 2 were waited for; matrix products, arithmetic and copies ran while one was open for 3% of the time, Pallas kernels for 43%

profile of v2, /device:TPU:1, one launch (start us, length us, event | category | flops | bytes accessed | tf_op | source)
XLA Modules:
  0.0 452.7 jit_solution(4091351229855005032)
XLA Ops:
  7.2 0.0 all-gather.2.cloned.1.call-start
  7.2 1.8 dynamic_update_slice.15.vec_ref
  9.0 0.6 copy-done.16
  9.6 64.2 %opening.1 = (bf16[1024,256]{1,0:T(8,128)(2,1)}, bf16[1024,256]{1,0:T(8,128)(2,1)}, bf16[1024,256]{1,0:T(8,128)(2,1)}, f32[1024,256]{1,0:T(8,128)}, f32[16,2048]...) custom-call(bf16[128,2048]{1,0:T(8,128)(2,1)} %bitcast.19, ...), custom_call_target="tpu_custom_call" | custom-call | bytes 180000000 | tf_op jit(solution)/shard_map/opening/pallas_call | solution.py:518
  73.9 0.0 reduce-scatter.2.cloned.1.call-start
  73.9 0.7 dynamic-slice_log_fusion
  74.7 0.1 broadcast_in_dim.25
  74.7 0.1 broadcast_in_dim_reshape.3
  74.8 0.1 pad.2.clone
  74.9 0.8 dynamic-slice
  75.7 0.1 maximum_maximum_fusion.p_ref.params_ref
  75.8 1.0 copy-done
  76.8 0.9 copy-done.1
  77.7 1.0 copy-done.3
  78.8 1.0 copy-done.4
  79.8 1.1 copy-done.5
  80.9 57.7 %recurrence.1 = (bf16[1024,256]{1,0:T(8,128)(2,1)S(1)}, f32[1024,256]{1,0:T(8,128)S(1)}, f32[1024,256]{1,0:T(8,128)S(1)}, bf16[16,64,256]{2,1,0:T(8,128)(2,1)S(1...) custom-call(bf16[1024,256]{1,0:T(8,128)(2,1)S(1)} %copy-done.3, ...), custom_call_target="tpu_custom_call" | custom-call | bytes 165000000 | tf_op jit(solution)/shard_map/recurrence/pallas_call | solution.py:242
  138.6 1.0 copy-done.6
  139.6 1.0 copy-done.7
  140.6 0.8 copy-done.8
  141.4 0.8 copy-done.9
  142.2 0.8 copy-done.10
  143.0 0.1 broadcast_compare_fusion
  143.1 0.9 broadcast_select_fusion
  144.0 3.1 all-gather.2.cloned.1.call-done.w_hbm
  147.0 132.8 %channel.1 = (bf16[128,2048]{1,0:T(8,128)(2,1)}, f32[128,2048]{1,0:T(8,128)}, f32[8,2048]{1,0:T(8,128)}, bf16[2048,2048]{1,0:T(8,128)(2,1)}) custom-call(bf16[128,2048]{1,0:T(8,128)(2,1)} %copy-done.10, f32[128,2048]{1,0:T(8,128)} %get-tuple-element.44.hidden_ref, bf16[128,2048]{1,0:T(8,128)(2,1)} %bitcast.27, ...), custom_call_target="tpu_custom_call" | custom-call | bytes 360000000 | tf_op jit(solution)/shard_map/channel/pallas_call | solution.py:913
  279.9 0.9 copy-done.2
  280.7 1.4 copy.16
  282.1 60.6 %middle.1 = (f32[128,2048]{1,0:T(8,128)}, bf16[4,1024,256]{2,1,0:T(8,128)(2,1)}, f32[8,2048]{1,0:T(8,128)}, f32[8,256]{1,0:T(8,128)}, bf16[2048,512]{1,0:T(8,128)(2,1)}) custom-call(f32[128,2048]{1,0:T(8,128)} %get-tuple-element.47.second_ref, f32[128,2048]{1,0:T(8,128)} %get-tuple-element.44.hidden_ref, bf16[128,2048]{1,0:T(8,128)(2,1)} %bitcast.28, ...), custom_call_target="tpu_custom_call" | custom-call | tf_op jit(solution)/shard_map/middle/pallas_call | solution.py:1135
  342.7 0.8 slice.39
  343.6 0.8 slice.35
  344.4 0.8 slice.40
  345.3 0.7 slice_dynamic-update-slice_fusion
  346.0 0.7 slice_dynamic-update-slice_fusion.1
  346.7 0.7 slice_dynamic-update-slice_fusion.2
  347.4 1.4 stack.14.vec_ref
  348.8 78.2 %closing.1 = (bf16[128,2048]{1,0:T(8,128)(2,1)}, f32[5,16,2048]{2,1,0:T(8,128)}, f32[16,128]{1,0:T(8,128)}) custom-call(bf16[4,1024,256]{2,1,0:T(8,128)(2,1)} %get-tuple-element.55.grad_ref, bf16[4,4,128,512]{3,2,1,0:T(8,128)(2,1)} %bitcast.29, bf16[5,2048,256]{2,1,0:T(8,128)(2,1)} %bitcast.24, bf16[1024,2048]{1,0:T(8,128)(2,1)} %get-tuple-element.52.prev_hbm, ...), custom_call_target="tpu_custom_call" | custom-call | tf_op jit(solution)/shard_map/closing/pallas_call | solution.py:1447
  427.1 3.9 all-to-all-start
  431.0 1.4 constant_dynamic-slice_fusion
  432.4 8.1 %all-to-all-done = bf16[8,16,2048]{2,1,0:T(8,128)(2,1)S(1)} async-done(((bf16[8,16,2048]{2,1,0:T(8,128)(2,1)}), bf16[8,16,2048]{2,1,0:T(8,128)(2,1)S(1)}, u32[]{:S(2)}, u32[]{:S(2)}) %all-to-all-start) | async-done | bytes 524320 | tf_op jit(solution)/shard_map/all_to_all | solution.py:1594
  440.5 0.1 convert_bitcast_fusion
  440.6 0.1 slice_bitcast_fusion
  440.7 0.8 copy.20
  441.5 0.8 copy.21
  442.3 0.7 copy.22
  443.0 0.8 copy.30
  443.8 0.8 copy.31
  444.6 0.8 copy.32
  (37 shorter events, 0.2 us)
Async XLA Ops:
  7.2 139.9 %all-gather.2.cloned.1.call-start = ((), (), s32[]{:S(2)}) async-start(), calls=%async_computation.2 | async-start | bytes 8912896 | tf_op jit(solution)/shard_map/all_gather | solution.py:1518
  9.0 0.6 copy-start.16
  73.9 353.2 %reduce-scatter.2.cloned.1.call-start = ((), (), s32[]{:S(2)}) async-start(), calls=%async_computation.3 | async-start | bytes 8912896 | tf_op jit(solution)/shard_map/reduce_scatter | solution.py:1537
  75.8 62.8 %copy-start.11 = (f32[8,256]{1,0:T(8,128)}, f32[8,256]{1,0:T(8,128)S(1)}, u32[]{:S(2)}) copy-start(f32[8,256]{1,0:T(8,128)S(1)} %maximum_maximum_fusion.p_ref.params_ref) | copy-start | bytes 24580
  75.8 1.0 copy-start
  76.8 0.9 copy-start.1
  77.7 1.0 copy-start.3
  78.8 1.0 copy-start.4
  79.8 1.1 copy-start.5
  80.9 62.1 %copy-start.17 = (s32[2]{0:T(128)S(1)}, s32[2]{0:T(128)}, u32[]{:S(2)}) copy-start(s32[2]{0:T(128)} %param.16) | copy-start | bytes 28
  80.9 62.2 %copy-start.15 = (bf16[2,64,2048]{2,1,0:T(8,128)(2,1)S(1)}, bf16[2,64,2048]{2,1,0:T(8,128)(2,1)}, u32[]{:S(2)}) copy-start(bf16[2,64,2048]{2,1,0:T(8,128)(2,1)} %param.17) | copy-start | bytes 1572868
  138.6 1.0 copy-start.6
  139.6 1.0 copy-start.7
  140.6 0.8 copy-start.8
  141.4 0.8 copy-start.9
  142.2 0.8 copy-start.10
  279.8 0.9 copy-start.2
  427.0 15.9 %copy-start.13 = (bf16[128,2048]{1,0:T(8,128)(2,1)S(1)}, bf16[128,2048]{1,0:T(8,128)(2,1)}, u32[]{:S(2)}) copy-start(bf16[128,2048]{1,0:T(8,128)(2,1)} %get-tuple-element.46) | copy-start | bytes 1572868
  427.0 16.7 %copy-start.14 = (bf16[128,2048]{1,0:T(8,128)(2,1)S(1)}, bf16[128,2048]{1,0:T(8,128)(2,1)}, u32[]{:S(2)}) copy-start(bf16[128,2048]{1,0:T(8,128)(2,1)} %get-tuple-element.61) | copy-start | bytes 1572868
  427.1 13.4 %all-to-all-start = ((bf16[8,16,2048]{2,1,0:T(8,128)(2,1)}), bf16[8,16,2048]{2,1,0:T(8,128)(2,1)S(1)}, u32[]{:S(2)}, u32[]{:S(2)}) async-start(bf16[8,16,2048]{2,1,0:T(8,128)(2,1)} %bitcast.31), calls=%async_computation.1 | async-start | bytes 1048576 | tf_op jit(solution)/shard_map/all_to_all | solution.py:1594
  431.0 13.6 %copy-start.12 = (f32[5,16,2048]{2,1,0:T(8,128)S(1)}, f32[5,16,2048]{2,1,0:T(8,128)}, u32[]{:S(2)}) copy-start(f32[5,16,2048]{2,1,0:T(8,128)} %get-tuple-element.78) | copy-start | bytes 1966084
Sparse Core Ops, SparseCore 0:
  74.0 73.0 all-gather.1
  280.0 90.6 reduce-scatter.1
